TPU v7x, 32 devices: a whole 2x2x4 slice. The times are simulated.
32 devices in a mesh: dp: 16 (over z, y, x), fsdp: 2 (over core).
Axes of the slice: x: 2, y: 2, z: 4, core: 2. Of those that a mesh axis runs over, the one named last changes fastest.
Arguments:
- tokens: bfloat16 [32, 1024, 512], P(('dp', 'fsdp')), may hold values from -6 to 6
- encoder: bfloat16 [32, 1024, 512], P(('dp', 'fsdp')), may hold values from -6 to 6
- out_grad: bfloat16 [32, 1024, 512], P(('dp', 'fsdp')), may hold values from -6 to 6
- self_qkv: bfloat16 [3, 512, 512], P(None, ('dp', 'fsdp')), may hold values from -0.25 to 0.25
- self_out: bfloat16 [512, 512], P(('dp', 'fsdp')), may hold values from -1 to 1
- cross_qkv: bfloat16 [3, 512, 512], P(None, ('dp', 'fsdp')), may hold values from -0.25 to 0.25
- cross_out: bfloat16 [512, 512], P(('dp', 'fsdp')), may hold values from -1 to 1
- ffn_in: bfloat16 [512, 2048], P(('dp', 'fsdp')), may hold values from -0.25 to 0.25
- ffn_out: bfloat16 [2048, 512], P(('dp', 'fsdp')), may hold values from -0.1875 to 0.1875
- ln_gain: bfloat16 [3, 512], P(None, ('dp', 'fsdp')), may hold values from 0.5 to 1.5
- ln_bias: bfloat16 [3, 512], P(None, ('dp', 'fsdp')), may hold values from -3 to 3
- tgt_lengths: int32 [32, 16], P(('dp', 'fsdp')), may hold values from 1 to 640, 1024 in all within a row
- tgt_pad: int32 [32], P(('dp', 'fsdp')), may hold values from 0 to 128
- src_segments: int32 [32, 1024], P(('dp', 'fsdp')), may hold values from 0 to 15, never falling along the last dimension, each value on 1 to 640 neighbouring positions
Outputs:
- out_tokens: bfloat16 [32, 1024, 512], P(('dp', 'fsdp'))
- tokens_grad: bfloat16 [32, 1024, 512], P(('dp', 'fsdp'))
- encoder_grad: bfloat16 [32, 1024, 512], P(('dp', 'fsdp'))
- self_qkv_grad: float32 [3, 512, 512], P(None, ('dp', 'fsdp'))
- self_out_grad: float32 [512, 512], P(('dp', 'fsdp'))
- cross_qkv_grad: float32 [3, 512, 512], P(None, ('dp', 'fsdp'))
- cross_out_grad: float32 [512, 512], P(('dp', 'fsdp'))
- ffn_in_grad: float32 [512, 2048], P(('dp', 'fsdp'))
- ffn_out_grad: float32 [2048, 512], P(('dp', 'fsdp'))
- ln_gain_grad: float32 [3, 512], P(None, ('dp', 'fsdp'))
- ln_bias_grad: float32 [3, 512], P(None, ('dp', 'fsdp'))
All inputs are finite; a program needn't handle non-finite values.
Results may differ from a plain program's by a relative error of at most 0.023.
The roundings to bfloat16 on the way count: a program that leaves them out, or rounds other values in their place, can miss the bound.
Values may be sent and summed in bfloat16 or wider, within the bound.
No kernel may reach another device: no remote copies, remote signals or barrier semaphores. Data moves between devices by JAX's collectives and lax.ppermute only.
A program may use at most 192 MiB of HBM per device.

v0:
```python
import math

import jax
import jax.numpy as jnp
from jax import lax
from jax.experimental import pallas as pl
from jax.experimental.pallas import tpu as pltpu
from jax.sharding import PartitionSpec as P

F32 = jnp.float32
BF16 = jnp.bfloat16
HEAD_DIM = 64
PAIR = 2 * HEAD_DIM
TILE = 128
BLOCK = 16
AXES = ("dp", "fsdp")
QUERY_SCALE = math.log2(math.e) / math.sqrt(HEAD_DIM)
MASK_ROWS = 32
MASKED = -1e30
WINDOWS = (2, 4, 6, 8)
SMEM = pl.BlockSpec(memory_space=pltpu.SMEM)
ANYWHERE = pl.BlockSpec(memory_space=pl.ANY)
HBM = pl.BlockSpec(memory_space=pltpu.HBM)
VMEM = pl.BlockSpec(memory_space=pltpu.VMEM)


def dot(left, right):
    return jnp.dot(left, right, preferred_element_type=F32)


def dot_tn(left, right):
    return lax.dot_general(left, right, (((0,), (0,)), ((), ())), preferred_element_type=F32)


def dot_nt(left, right):
    return lax.dot_general(left, right, (((1,), (1,)), ((), ())), preferred_element_type=F32)


def iota(shape, axis):
    return lax.broadcasted_iota(jnp.int32, shape, axis)


def part_shape(shape, index):
    if index is None:
        return shape
    index = index if isinstance(index, tuple) else (index,)
    taken = [one.stop - one.start for one in index if isinstance(one, slice)]
    return (*taken, *shape[len(index) :])


class Copies:

    def __init__(self, semaphores):
        self.semaphores = semaphores
        self.used = 0
        self.coming = {}
        self.going = {}
        self.started = []

    def start(self, source, target):
        copy = pltpu.make_async_copy(source, target, self.semaphores.at[self.used])
        self.used += 1
        copy.start()
        return copy

    def need(self, *refs):
        for ref in refs:
            self.coming.pop(id(ref)).wait()

    def push(self, *refs):
        for ref in refs:
            self.started.append(self.start(ref, self.going.pop(id(ref))))

    def push_part(self, source, target):
        self.started.append(self.start(source, target))

    def finish(self):
        for copy in self.coming.values():
            copy.wait()
        for copy in self.started:
            copy.wait()


def call(body, name, outs, ins, in_smem, micros, scratch=(), out_smem=(), after=(), by_part=(), near=(), limit=58):
    ins = [one if isinstance(one, tuple) else (one, None) for one in ins]
    indexes = [index for _, index in ins]
    ins = [array for array, _ in ins]
    in_count, out_count = len(ins), len(outs)
    moved_in = [at for at in range(in_count) if at not in in_smem and at not in near]
    moved_out = [at for at in range(out_count) if at not in out_smem and at not in by_part]

    def ordered(*refs):
        sources, refs = list(refs[:in_count]), refs[in_count + len(after) :]
        targets, refs = list(refs[:out_count]), refs[out_count:]
        buffers_in, refs = refs[: len(moved_in)], refs[len(moved_in) :]
        buffers_out, refs = refs[: len(moved_out)], refs[len(moved_out) :]
        copies = Copies(refs[0])
        for at, buffer in zip(moved_in, buffers_in):
            source = sources[at] if indexes[at] is None else sources[at].at[indexes[at]]
            copies.coming[id(buffer)] = copies.start(source, buffer)
            sources[at] = buffer
        for at, buffer in zip(moved_out, buffers_out):
            copies.going[id(buffer)] = targets[at]
            targets[at] = buffer
        body(copies, *sources, *targets, *refs[1:])
        copies.finish()

    return pl.pallas_call(
        ordered,
        name=name,
        out_shape=[jax.ShapeDtypeStruct(shape, kind) for shape, kind in outs],
        in_specs=[SMEM if at in in_smem else VMEM if at in near else HBM for at in range(in_count)] + [ANYWHERE] * len(after),
        out_specs=[SMEM if at in out_smem else HBM for at in range(out_count)],
        scratch_shapes=[pltpu.VMEM(part_shape(ins[at].shape, indexes[at]), ins[at].dtype) for at in moved_in]
        + [pltpu.VMEM(*outs[at]) for at in moved_out]
        + [pltpu.SemaphoreType.DMA((len(moved_in) + len(moved_out) + 4 * len(by_part),))]
        + [pltpu.VMEM(shape, kind) for shape, kind in scratch],
        compiler_params=pltpu.CompilerParams(vmem_limit_bytes=limit * 2**20),
        cost_estimate=pl.CostEstimate(flops=int(micros * 1e9), bytes_accessed=0, transcendentals=0),
    )(*ins, *after)


def call_near(body, name, outs, ins, micros, after=()):
    count = len(ins)
    return pl.pallas_call(
        lambda *refs: body(*refs[:count], *refs[count + len(after) :]),
        name=name,
        out_shape=[jax.ShapeDtypeStruct(shape, kind) for shape, kind in outs],
        in_specs=[VMEM] * count + [ANYWHERE] * len(after),
        out_specs=[VMEM] * len(outs),
        compiler_params=pltpu.CompilerParams(vmem_limit_bytes=16 * 2**20),
        cost_estimate=pl.CostEstimate(flops=int(micros * 1e9), bytes_accessed=0, transcendentals=0),
    )(*ins, *after)


def prep_body(copies, lengths, padding, src_grid, src_column, self_kaug, self_qaug, cross_kaug, cross_qaug, windows, zero):
    zero[0] = 0
    copies.need(src_grid, src_column)
    rows = self_kaug.shape[0]
    count = lengths.shape[0]
    edge = rows - padding[0]
    ends, total = [], 0
    for at in range(count):
        total = total + lengths[at]
        ends.append(total)

    def labels(places):
        found = sum((places >= end).astype(jnp.int32) for end in ends)
        return jnp.where(places < edge, found, count)

    row_ids = labels(iota((8, rows), 1))[0:1]
    mask_rows = iota((MASK_ROWS, rows), 0)
    self_qaug[...] = jnp.where(row_ids != mask_rows, 1.0, 0.0).astype(BF16)
    cross_qaug[...] = jnp.where(jnp.minimum(row_ids, count - 1) != mask_rows, 1.0, 0.0).astype(BF16)
    lanes = iota((TILE, TILE), 1)
    ones_lanes = jnp.where((lanes >= MASK_ROWS) & (lanes < MASK_ROWS + 3), 1.0, 0.0)
    for tile in range(rows // TILE):
        part = slice(tile * TILE, (tile + 1) * TILE)
        column_ids = labels(iota((TILE, TILE), 0) + tile * TILE)
        self_kaug[part, :] = jnp.where(column_ids == lanes, MASKED, ones_lanes).astype(BF16)
        cross_kaug[part, :] = jnp.where(src_column[part, :] == lanes, MASKED, ones_lanes).astype(BF16)
    copies.push(self_kaug, self_qaug, cross_kaug, cross_qaug)
    for tile in range(rows // TILE):
        first, last = tile * TILE, tile * TILE + TILE - 1
        start, stop, first_id, last_id = 0, edge, 0, 0
        for end in ends:
            start = jnp.where(end <= first, end, start)
            first_id = first_id + jnp.where(end <= first, 1, 0)
            last_id = last_id + jnp.where(end <= last, 1, 0)
        for end in reversed(ends):
            stop = jnp.where(end > last, jnp.minimum(end, edge), stop)
        start = jnp.where(first >= edge, edge, start)
        stop = jnp.where(last >= edge, rows, stop)
        first_id = jnp.where(first < edge, jnp.minimum(first_id, count - 1), count - 1)
        last_id = jnp.where(last < edge, jnp.minimum(last_id, count - 1), count - 1)
        low = start // TILE
        windows[0, tile] = low
        windows[1, tile] = (stop + TILE - 1) // TILE - low
        source = src_grid[...]
        below = jnp.sum(jnp.where(source < first_id, 1, 0))
        upto = jnp.sum(jnp.where(source <= last_id, 1, 0))
        low = below // TILE
        windows[2, tile] = low
        windows[3, tile] = (upto + TILE - 1) // TILE - low


def pair_columns(block):
    upper = iota(block.shape, 0) < HEAD_DIM
    none = jnp.zeros_like(block)
    return jnp.concatenate([jnp.where(upper, block, none), jnp.where(upper, none, block)], axis=1)


def pair_rows(block):
    left = iota(block.shape, 1) < HEAD_DIM
    none = jnp.zeros_like(block)
    return jnp.concatenate([jnp.where(left, block, none), jnp.where(left, none, block)], axis=0)


def twice(block):
    return jnp.concatenate([block, block], axis=1)


def split_three(row):
    first = row.astype(BF16).astype(F32)
    second = (row - first).astype(BF16).astype(F32)
    third = row - first - second
    at = iota((BLOCK, row.shape[1]), 0)
    none = jnp.zeros((BLOCK, row.shape[1]), F32)
    picked = jnp.where(at == 0, first, jnp.where(at == 1, second, jnp.where(at == 2, third, none)))
    return picked.astype(BF16)


def over_windows(windows, row, rows, run):
    tiles = rows // TILE

    def one_tile(tile, _):
        low, width = windows[row, tile], windows[row + 1, tile]
        before = 0
        for most in WINDOWS:
            start = jnp.minimum(low, tiles - most) * TILE

            @pl.when((width > before) & (width <= most))
            def _():
                run(pl.multiple_of(tile * TILE, TILE), pl.multiple_of(start, TILE), most * TILE)

            before = most
        return 0

    lax.fori_loop(0, tiles, one_tile, 0)


def places(pair):
    inner = (pair % 2) * PAIR
    return pair // 2, slice(inner, inner + PAIR)


def head_places(pair, head):
    inner = (pair % 2) * PAIR + head * HEAD_DIM
    return pair // 2, slice(inner, inner + HEAD_DIM), slice((pair % 2) * 2 + head, (pair % 2) * 2 + head + 1)


def attend(windows, row, queries_t, keys, values_t, kaug, qaug, mixed_t, log_mass, scores, raised):
    halves, rows, width = keys.shape
    pairs = halves * width // PAIR

    def run(query_at, key_at, key_count):
        query_part, key_part = pl.ds(query_at, TILE), pl.ds(key_at, key_count)
        mask_part = twice(qaug[:, query_part])
        empty = jnp.zeros((PAIR - MASK_ROWS, 2 * TILE), BF16)
        ones = jnp.ones((BLOCK, key_count), BF16)
        rights, found, peaks = [], [None] * pairs, [None] * pairs
        for pair in range(pairs):
            half, part = places(pair)
            rights.append(jnp.concatenate([pair_columns(queries_t[half, part, query_part]), mask_part, empty], axis=0))

        def score(pair, at):
            half, part = places(pair)
            here, span = pl.ds(key_at + at, TILE * 2), slice(at, at + TILE * 2)
            value = dot(jnp.concatenate([keys[half, here, part], kaug[here, :]], axis=1), rights[pair])
            scores[pair % 2, span, :] = value
            most = jnp.max(value.reshape(-1, 8, 2 * TILE), axis=0)
            found[pair] = most if at == 0 else jnp.maximum(found[pair], most)

        def raise_up(pair, at):
            span = slice(at, at + TILE * 2)
            if at == 0:
                peaks[pair] = jnp.max(found[pair], axis=0, keepdims=True)
            raised[pair % 2, span, :] = jnp.exp2(scores[pair % 2, span, :] - peaks[pair]).astype(BF16)

        def mix(pair):
            half, part = places(pair)
            left = jnp.concatenate([values_t[half, part, key_part], ones], axis=0)
            mixed = dot(left, raised[pair % 2, 0:key_count, :])
            mass = mixed[PAIR : PAIR + 1]
            scale = 1.0 / mass
            logs = peaks[pair] + jnp.log2(mass)
            for head in range(2):
                spot = slice(head * TILE, (head + 1) * TILE)
                inner = slice(head * HEAD_DIM, (head + 1) * HEAD_DIM)
                half, outer, at = head_places(pair, head)
                mixed_t[half, outer, query_part] = (mixed[inner, spot] * scale[:, spot]).astype(BF16)
                log_mass[half, at, query_part] = logs[:, spot]

        for step in range(pairs + 2):
            for at in range(0, key_count, TILE * 2):
                if step < pairs:
                    score(step, at)
                if 0 <= step - 1 < pairs:
                    raise_up(step - 1, at)
                if at == 0 and 0 <= step - 2 < pairs:
                    mix(step - 2)

    over_windows(windows, row, rows, run)


def attend_back(
    windows, row, queries, queries_t, keys, keys_t, values, kaug, qaug, log_mass, delta, grad, grad_t,
    query_grad_t, key_grad, value_grad,
):
    halves, rows, width = keys.shape
    key_grad[...] = jnp.zeros_like(key_grad)
    value_grad[...] = jnp.zeros_like(value_grad)

    def run(query_at, key_at, key_count):
        query_part, key_part = pl.ds(query_at, TILE), pl.ds(key_at, key_count)
        mask_part = twice(qaug[:, query_part])
        no_mask = jnp.zeros((MASK_ROWS, 2 * TILE), BF16)
        empty = jnp.zeros((PAIR - MASK_ROWS - BLOCK, 2 * TILE), BF16)
        key_mask = kaug[key_part, :]
        for pair in range(halves * width // PAIR):
            half, part = places(pair)
            heads = [head_places(pair, head) for head in range(2)]
            masses = jnp.concatenate([log_mass[half, at, query_part] for half, _, at in heads], axis=1)
            deltas = jnp.concatenate([delta[half, at, query_part] for half, _, at in heads], axis=1)
            right = jnp.concatenate(
                [pair_columns(queries_t[half, part, query_part]), mask_part, split_three(-masses), empty], axis=0
            )
            probs = jnp.exp2(dot(jnp.concatenate([keys[half, key_part, part], key_mask], axis=1), right))
            right = jnp.concatenate(
                [pair_columns(grad_t[half, part, query_part]), no_mask, split_three(-deltas), empty], axis=0
            )
            grad_probs = dot(jnp.concatenate([values[half, key_part, part], key_mask], axis=1), right)
            grad_scores = (probs * grad_probs).astype(BF16)
            value_grad[half, key_part, part] += dot(probs.astype(BF16), pair_rows(grad[half, query_part, part]))
            key_grad[half, key_part, part] += dot(grad_scores, pair_rows(queries[half, query_part, part]))
            mixed = dot(keys_t[half, part, key_part], grad_scores)
            for head, (half, outer, _) in enumerate(heads):
                spot = slice(head * TILE, (head + 1) * TILE)
                inner = slice(head * HEAD_DIM, (head + 1) * HEAD_DIM)
                query_grad_t[half, outer, query_part] = mixed[inner, spot]

    over_windows(windows, row, rows, run)


def row_deltas(mixed_t, grad_t, delta):
    halves, width, rows = mixed_t.shape
    for half in range(halves):
        for head in range(width // HEAD_DIM):
            part = slice(head * HEAD_DIM, (head + 1) * HEAD_DIM)
            product = mixed_t[half, part, :].astype(F32) * grad_t[half, part, :].astype(F32)
            delta[half, head : head + 1, :] = jnp.sum(product, axis=0, keepdims=True)


def normalize(hidden):
    center = hidden - jnp.mean(hidden, axis=-1, keepdims=True)
    spread = jnp.mean(center * center, axis=-1, keepdims=True)
    inverse = lax.rsqrt(spread + 1e-05)
    return center * inverse, inverse


def normalize_back(incoming, normal, inverse, gain):
    scaled = incoming * gain
    average = jnp.mean(scaled, axis=-1, keepdims=True)
    along = jnp.mean(scaled * normal, axis=-1, keepdims=True)
    return inverse * (scaled - average - normal * along)


def chunks(rows, step, run):
    def one(at, _):
        run(pl.ds(pl.multiple_of(at * step, step), step))
        return 0

    lax.fori_loop(0, rows // step, one, 0)


def fold_rows(block):
    return jnp.sum(block.reshape(-1, 8, block.shape[1]), axis=0)


def mirrored(number):
    return sum(((number >> bit) & 1) << (4 - bit) for bit in range(5))


def origin(spots, spot):
    return jnp.where(spots[0] == 1, mirrored(spot) ^ spots[1], spot)


def place(spots, block):
    return jnp.where(spots[0] == 1, mirrored(block) ^ spots[2], block)


def take_blocks(spots, low, high, row, target):
    half = low.shape[0]
    for spot in range(2 * half):
        source = low if spot < half else high
        start = pl.multiple_of(origin(spots, spot) * BLOCK, BLOCK)
        target[pl.ds(start, BLOCK), :] = source[spot % half, row : row + BLOCK, :]


def put_blocks(spots, grads, first, rows_each, row, value):
    for at in range(value.shape[0] // rows_each):
        grads[place(spots, first + at), row : row + rows_each, :] = value[at * rows_each : (at + 1) * rows_each]


def hand_out(copies, grads, keep, send):
    half = keep.shape[0]
    copies.push_part(grads.at[half : 2 * half], send)
    copies.push_part(grads.at[0:half], keep)


def pack_body(copies, self_qkv, self_out, cross_qkv, cross_out, ffn_in, ffn_out, gain, offset, self_block, cross_block, ffn_block):
    copies.need(self_qkv, self_out, cross_qkv, cross_out, ffn_in, ffn_out, gain, offset)
    width = self_out.shape[1]
    own = gain.shape[1]
    for which in range(3):
        rows = slice(which * BLOCK, (which + 1) * BLOCK)
        self_block[0, rows, :] = self_qkv[which]
        cross_block[0, rows, :] = cross_qkv[which]
    cross_block[0, 3 * BLOCK : 4 * BLOCK, :] = cross_out[...]
    cross_block[0, 4 * BLOCK : 5 * BLOCK, :] = self_out[...]
    scales = jnp.concatenate([gain[...].astype(F32), offset[...].astype(F32), jnp.zeros((BLOCK - 6, own), F32)], axis=0)
    scales = jnp.concatenate([scales, jnp.zeros((BLOCK, width - own), F32)], axis=1)
    cross_block[0, 5 * BLOCK : 6 * BLOCK, :] = scales.astype(BF16)
    parts = ffn_in.shape[1] // width
    for part in range(parts):
        ffn_block[part * BLOCK : (part + 1) * BLOCK, :] = ffn_in[:, part * width : (part + 1) * width]
    ffn_block[parts * BLOCK :, :] = ffn_out[...]
    copies.push(self_block, cross_block, ffn_block)


def lay_rows(value, target, part):
    wide = target.shape[2]
    for half in range(target.shape[0]):
        target[half, part, :] = value[:, half * wide : (half + 1) * wide]


def lay_columns(value, target, part):
    wide = target.shape[1]
    turned = value.T
    for half in range(target.shape[0]):
        target[half, :, part] = turned[half * wide : (half + 1) * wide]


def mixed_product(mixed_t, part, weight):
    wide = mixed_t.shape[1]
    return sum(dot_tn(mixed_t[half, :, part], weight[half * wide : (half + 1) * wide, :]) for half in range(mixed_t.shape[0]))


def self_forward_body(
    copies, low, high, tokens, kaug, qaug, spots, windows,
    queries, queries_t, keys, keys_t, values, mixed_t, log_mass, weights, zero,
    values_t, scores, raised,
):
    zero[0] = 0
    for which in range(3):
        take_blocks(spots, low, high, which * BLOCK, weights.at[which])
    copies.push(weights)
    copies.need(tokens)

    def project(part):
        rows = tokens[part, :]
        query_rows = (dot(rows, weights[0]) * QUERY_SCALE).astype(BF16)
        lay_rows(query_rows, queries, part)
        lay_columns(query_rows, queries_t, part)
        key_rows = dot(rows, weights[1]).astype(BF16)
        lay_rows(key_rows, keys, part)
        lay_columns(key_rows, keys_t, part)
        value_rows = dot(rows, weights[2]).astype(BF16)
        lay_rows(value_rows, values, part)
        lay_columns(value_rows, values_t, part)

    chunks(tokens.shape[0], 256, project)
    copies.push(queries, queries_t, keys, keys_t, values)
    copies.need(kaug, qaug)
    attend(windows, 0, queries_t, keys, values_t, kaug, qaug, mixed_t, log_mass, scores, raised)
    copies.push(mixed_t, log_mass)


def cross_forward_body(
    copies, low, high, tokens, self_mixed_t, encoder, kaug, qaug, spots, windows,
    hidden, hidden_two, first_low, queries, queries_t, keys, keys_t, values, mixed_t, log_mass, weights, scales,
    values_t, scores, raised, first,
):
    for which in range(5):
        take_blocks(spots, low, high, which * BLOCK, weights.at[which])
    half = low.shape[0]
    gathered = jnp.zeros(scales.shape, F32)
    for spot in range(2 * half):
        source = low if spot < half else high
        block = source[spot % half, 5 * BLOCK : 6 * BLOCK, :].astype(F32)
        gathered = gathered + pltpu.roll(block, origin(spots, spot) * BLOCK, 1)
    scales[...] = gathered
    copies.push(weights, scales)
    gain, offset = scales[0:1, :], scales[3:4, :]
    copies.need(tokens, self_mixed_t, encoder)

    def project(part):
        rows = encoder[part, :]
        key_rows = dot(rows, weights[1]).astype(BF16)
        lay_rows(key_rows, keys, part)
        lay_columns(key_rows, keys_t, part)
        value_rows = dot(rows, weights[2]).astype(BF16)
        lay_rows(value_rows, values, part)
        lay_columns(value_rows, values_t, part)
        before = tokens[part, :].astype(F32) + mixed_product(self_mixed_t, part, weights.at[4])
        hidden[part, :] = before
        normal, _ = normalize(before)
        first_rows = normal * gain + offset
        first[part, :] = first_rows
        low_rows = first_rows.astype(BF16)
        first_low[part, :] = low_rows
        query_rows = (dot(low_rows, weights[0]) * QUERY_SCALE).astype(BF16)
        lay_rows(query_rows, queries, part)
        lay_columns(query_rows, queries_t, part)

    chunks(encoder.shape[0], 256, project)
    copies.push(hidden, first_low, queries, queries_t, keys, keys_t, values)
    copies.need(kaug, qaug)
    attend(windows, 2, queries_t, keys, values_t, kaug, qaug, mixed_t, log_mass, scores, raised)
    copies.push(mixed_t, log_mass)

    def finish(part):
        hidden_two[part, :] = first[part, :] + mixed_product(mixed_t, part, weights.at[3])

    chunks(encoder.shape[0], 256, finish)
    copies.push(hidden_two)


def feed_forward_body(
    copies, gathered, hidden, out_grad, scales, cross_mixed_t, spots,
    out, grad_two, scale_grads, weight_grads,
    inner, outer, inner_t, outer_t, second_low, active, slope, branch, grad_inner, cross_branch, sums, grads,
):
    rows, width = hidden.shape
    wide = outer.shape[0]
    parts = wide // width
    each = wide // (width // BLOCK)
    copies.need(gathered)
    for block in range(width // BLOCK):
        for part in range(parts):
            inner[block * BLOCK : (block + 1) * BLOCK, part * width : (part + 1) * width] = gathered[
                block, part * BLOCK : (part + 1) * BLOCK, :
            ]
        outer[block * each : (block + 1) * each, :] = gathered[block, parts * BLOCK : parts * BLOCK + each, :]
    for part in range(parts):
        span = slice(part * width, (part + 1) * width)
        inner_t[span, :] = inner[:, span].T
        outer_t[:, span] = outer[span, :].T
    sums[...] = jnp.zeros_like(sums)
    root = math.sqrt(2.0 / math.pi)
    copies.need(hidden, out_grad, scales)

    def one(part):
        normal_two, inverse_two = normalize(hidden[part, :])
        second = normal_two * scales[1:2, :] + scales[4:5, :]
        low = second.astype(BF16)
        second_low[part, :] = low
        for at in range(parts):
            span = slice(at * width, (at + 1) * width)
            value = dot(low, inner[:, span])
            square = value * value
            curve = jnp.tanh(root * (value + 0.044715 * (value * square)))
            active[part, span] = (0.5 * value * (1.0 + curve)).astype(BF16)
            slope[:, span] = 0.5 * (1.0 + curve) + (0.5 * root) * value * (1.0 - curve * curve) * (1.0 + 0.134145 * square)
        normal_three, inverse_three = normalize(second + dot(active[part, :], outer[...]))
        out[part, :] = (normal_three * scales[2:3, :] + scales[5:6, :]).astype(BF16)
        incoming = out_grad[part, :].astype(F32)
        sums[2] += fold_rows(incoming * normal_three)
        sums[5] += fold_rows(incoming)
        grad_three = normalize_back(incoming, normal_three, inverse_three, scales[2:3, :])
        grad_low = grad_three.astype(BF16)
        branch[part, :] = grad_low
        for at in range(parts):
            span = slice(at * width, (at + 1) * width)
            grad_inner[part, span] = (dot(grad_low, outer_t[:, span]) * slope[:, span]).astype(BF16)
        grad_second = grad_three + dot(grad_inner[part, :], inner_t[...])
        sums[1] += fold_rows(grad_second * normal_two)
        sums[4] += fold_rows(grad_second)
        result = normalize_back(grad_second, normal_two, inverse_two, scales[1:2, :])
        grad_two[part, :] = result
        cross_branch[part, :] = result.astype(BF16)

    chunks(rows, 256, one)
    scale_grads[...] = jnp.sum(sums[...], axis=1)
    copies.push(out, grad_two, scale_grads)
    inside = parts * BLOCK

    def put(first, rows_each, row, value):
        for at in range(value.shape[0] // rows_each):
            block = first + at
            spot = jnp.where(spots[0] == 1, (block % 8) * 4 + block // 8, block)
            grads[spot, row : row + rows_each, :] = value[at * rows_each : (at + 1) * rows_each]

    for at in range(parts):
        span = slice(at * width, (at + 1) * width)
        put(at * width // each, each, inside + BLOCK, dot_tn(active[:, span], branch[...]).astype(BF16))
    for at in range(parts):
        span = slice(at * width, (at + 1) * width)
        put(0, BLOCK, at * BLOCK, dot_tn(second_low[...], grad_inner[:, span]).astype(BF16))
    copies.push_part(grads.at[:, 0:inside, :], weight_grads.at[:, 0:inside, :])
    copies.push_part(grads.at[:, inside + BLOCK :, :], weight_grads.at[:, inside + BLOCK :, :])
    copies.need(cross_mixed_t)
    half_width = cross_mixed_t.shape[1]
    for half in range(cross_mixed_t.shape[0]):
        put(half * half_width // BLOCK, BLOCK, inside, dot(cross_mixed_t[half], cross_branch[...]).astype(BF16))
    copies.push_part(grads.at[:, inside : inside + BLOCK, :], weight_grads.at[:, inside : inside + BLOCK, :])


def back_projections(grad_rows, weight, grad, grad_t):
    def one(part):
        value = dot_nt(grad_rows[part, :], weight[...]).astype(BF16)
        lay_rows(value, grad, part)
        lay_columns(value, grad_t, part)

    chunks(grad.shape[1], 256, one)


def round_grads(query_grad_t, key_grad, value_grad, query_low, key_low, value_low):
    def one(part):
        for half in range(key_low.shape[0]):
            query_low[half, part, :] = (query_grad_t[half, :, part] * HEAD_DIM**-0.5).T.astype(BF16)
            key_low[half, part, :] = (key_grad[half, part, :] * math.log(2.0)).astype(BF16)
            value_low[half, part, :] = value_grad[half, part, :].astype(BF16)

    chunks(key_low.shape[1], 256, one)


def back_product(low, part, weight):
    wide = low.shape[2]
    return sum(dot_nt(low[half, part, :], weight[:, half * wide : (half + 1) * wide]) for half in range(low.shape[0]))


def weight_grad(spots, grads, row, left, low):
    wide = low.shape[2]
    for half in range(low.shape[0]):
        value = dot_tn(left[...], low[half]).astype(BF16)
        span = slice(half * wide, (half + 1) * wide)
        for at in range(value.shape[0] // BLOCK):
            grads[place(spots, at), row : row + BLOCK, span] = value[at * BLOCK : (at + 1) * BLOCK]


def cross_backward_body(
    copies, grad_two, out_weight, mixed_t, queries_t, keys, kaug, qaug, values, log_mass, queries, keys_t,
    query_weight, scales, hidden, first_low, encoder, self_mixed_t, scale_grads, windows, spots,
    grad_one, self_branch, key_low, value_low, keep, send,
    branch, query_low, grad, grad_t, delta, query_grad_t, key_grad, value_grad, sums, grads,
):
    rows, width = hidden.shape
    copies.need(grad_two, out_weight)

    def prepare(part):
        branch[part, :] = grad_two[part, :].astype(BF16)

    chunks(rows, 256, prepare)
    back_projections(branch, out_weight, grad, grad_t)
    copies.need(mixed_t)
    row_deltas(mixed_t, grad_t, delta)
    copies.need(queries_t, keys, kaug, qaug, values, log_mass, queries, keys_t)
    attend_back(
        windows, 2, queries, queries_t, keys, keys_t, values, kaug, qaug, log_mass, delta, grad, grad_t,
        query_grad_t, key_grad, value_grad,
    )
    round_grads(query_grad_t, key_grad, value_grad, query_low, key_low, value_low)
    copies.push(key_low, value_low)
    copies.need(query_weight, scales, hidden)
    sums[...] = jnp.zeros_like(sums)

    def finish(part):
        normal, inverse = normalize(hidden[part, :])
        incoming = grad_two[part, :] + back_product(query_low, part, query_weight)
        sums[0] += fold_rows(incoming * normal)
        sums[1] += fold_rows(incoming)
        result = normalize_back(incoming, normal, inverse, scales[0:1, :])
        grad_one[part, :] = result
        self_branch[part, :] = result.astype(BF16)

    chunks(rows, 256, finish)
    copies.push(self_branch, grad_one)
    copies.need(first_low, encoder, self_mixed_t, scale_grads)
    weight_grad(spots, grads, 0, first_low, query_low)
    weight_grad(spots, grads, BLOCK, encoder, key_low)
    weight_grad(spots, grads, 2 * BLOCK, encoder, value_low)
    half_width = self_mixed_t.shape[1]
    for half in range(self_mixed_t.shape[0]):
        value = dot(self_mixed_t[half], self_branch[...]).astype(BF16)
        put_blocks(spots, grads, half * half_width // BLOCK, BLOCK, 3 * BLOCK, value)
    at = iota((BLOCK, width), 0)
    own = jnp.sum(sums[...], axis=1)
    below = jnp.concatenate([scale_grads[...], jnp.zeros_like(scale_grads)], axis=0)
    every = jnp.where(at == 0, own[0:1], jnp.where(at == 3, own[1:2], below))
    for block in range(width // BLOCK):
        shift = (width - block * BLOCK) % width
        turned = every if shift == 0 else pltpu.roll(every, shift, 1)
        grads[place(spots, block), 4 * BLOCK : 5 * BLOCK, :] = turned.astype(BF16)
    hand_out(copies, grads, keep, send)


def self_backward_body(
    copies, branch, weight, mixed_t, queries_t, keys, kaug, qaug, values, log_mass, queries, keys_t, tokens, windows, spots,
    query_low, key_low, value_low, keep, send,
    grad, grad_t, delta, query_grad_t, key_grad, value_grad, grads,
):
    copies.need(branch, weight)
    back_projections(branch, weight, grad, grad_t)
    copies.need(mixed_t)
    row_deltas(mixed_t, grad_t, delta)
    copies.need(queries_t, keys, kaug, qaug, values, log_mass, queries, keys_t)
    attend_back(
        windows, 0, queries, queries_t, keys, keys_t, values, kaug, qaug, log_mass, delta, grad, grad_t,
        query_grad_t, key_grad, value_grad,
    )
    round_grads(query_grad_t, key_grad, value_grad, query_low, key_low, value_low)
    copies.push(query_low, key_low, value_low)
    copies.need(tokens)
    for which, low in enumerate((query_low, key_low, value_low)):
        weight_grad(spots, grads, which * BLOCK, tokens, low)
    hand_out(copies, grads, keep, send)


def encoder_grad_body(copies, key_low, value_low, weights, encoder_grad):
    copies.need(key_low, value_low, weights)

    def one(part):
        value = back_product(key_low, part, weights.at[0]) + back_product(value_low, part, weights.at[1])
        encoder_grad[part, :] = value.astype(BF16)

    chunks(encoder_grad.shape[0], 256, one)
    copies.push(encoder_grad)


def tokens_grad_body(copies, grad_one, weights, query_low, key_low, value_low, tokens_grad):
    copies.need(grad_one, weights, query_low, key_low, value_low)

    def one(part):
        value = grad_one[part, :]
        for which, low in enumerate((query_low, key_low, value_low)):
            value = value + back_product(low, part, weights.at[which])
        tokens_grad[part, :] = value.astype(BF16)

    chunks(grad_one.shape[0], 256, one)
    copies.push(tokens_grad)


def fold_body(groups, *refs):
    count = sum(2 * len(terms) for terms, _ in groups)
    terms_refs, results = list(refs[:count]), list(refs[count:])
    for terms, axis in groups:
        keep, send = results.pop(0), results.pop(0)
        for row, column in terms:
            kept, came = terms_refs.pop(0), terms_refs.pop(0)
            lead, (high, wide) = kept.shape[:-2], kept.shape[-2:]
            for number in range(math.prod(lead)):
                index, left = [], number
                for size in reversed(lead):
                    index.insert(0, left % size)
                    left //= size
                value = (kept[tuple(index)].astype(F32) + came[tuple(index)].astype(F32)).astype(BF16)
                target = keep if index.pop(axis) == 0 else send
                target[(*index, slice(row, row + high), slice(column, column + wide))] = value


def total_body(keep, came, cross_qkv, self_out, gain, offset, self_qkv):
    def total(first, rows):
        return keep[first : first + rows, :].astype(F32) + came[first : first + rows, :].astype(F32)

    for which in range(3):
        cross_qkv[which] = total(which * BLOCK, BLOCK)
        self_qkv[which] = total((5 + which) * BLOCK, BLOCK)
    self_out[...] = total(3 * BLOCK, BLOCK)
    scales = total(4 * BLOCK, BLOCK)
    gain[...] = scales[0:3, : gain.shape[1]]
    offset[...] = scales[3:6, : offset.shape[1]]


def exchange(value, bit, devices):
    with jax.named_scope("across_" + ("core", "x", "y", "z", "zz")[bit] if bit < 5 else "across"):
        return exchange_bit(value, bit, devices)


def exchange_bit(value, bit, devices):
    return lax.ppermute(value, AXES, [(at, at ^ (1 << bit)) for at in range(devices)])


def bit_count(devices):
    return devices.bit_length() - 1


def join(first, second, zero):
    both = jnp.concatenate([first, jnp.zeros_like(second)], axis=0)
    return lax.dynamic_update_slice(both, second, (first.shape[0] + zero, 0, 0))


def gather_blocks(block, devices, zero):
    held = block
    for bit in reversed(range(2, bit_count(devices))):
        held = jnp.concatenate([held, exchange(held, bit, devices)], axis=0)
    held = join(held, exchange(held, 1, devices), zero)
    return held, exchange(held, 0, devices)


def gather_plain(block, per, blocks):
    every = lax.all_gather(block, AXES, axis=0, tiled=False)
    parts = every.shape[1] // per
    every = every.reshape(every.shape[0], parts, per, every.shape[2]).transpose(1, 0, 2, 3)
    every = every.reshape(parts, blocks, -1, every.shape[3]).transpose(1, 0, 2, 3)
    every = every.reshape(blocks, -1, every.shape[3])
    return every[: blocks // 2], every[blocks // 2 :]


def fold(name, groups, after=()):
    ins, outs, shapes = [], [], []
    for terms, axis in groups:
        high = max(row + kept.shape[-2] for kept, _, row, _ in terms)
        wide = max(column + kept.shape[-1] for kept, _, _, column in terms)
        lead = list(terms[0][0].shape[:-2])
        lead.pop(axis)
        for kept, came, _, _ in terms:
            ins += [kept, came]
        outs += [((*lead, high, wide), BF16)] * 2
        shapes.append(([(row, column) for _, _, row, column in terms], axis))
    results = call_near(lambda *refs: fold_body(shapes, *refs), name, outs, ins, 2, after)
    return [tuple(results[at : at + 2]) for at in range(0, len(results), 2)]


def local(
    tokens, encoder, out_grad, self_qkv, self_out, cross_qkv, cross_out, ffn_in, ffn_out, ln_gain, ln_bias,
    tgt_lengths, tgt_pad, src_segments,
):
    devices = lax.axis_size("dp") * lax.axis_size("fsdp")
    me = lax.axis_index(AXES)
    token_rows, encoder_rows = tokens[0], encoder[0]
    rows, width = token_rows.shape
    wide = ffn_in.shape[1]
    own = self_out.shape[0]
    blocks = width // BLOCK
    direct = devices == blocks and devices == 32
    parts = wide // width
    each = wide // blocks
    heads = width // HEAD_DIM

    number = me.astype(jnp.int32)
    if direct:
        spots = jnp.stack([jnp.int32(1), number, mirrored(number)])
    else:
        spots = jnp.zeros((3,), jnp.int32)

    square, tall = (rows, width), (width, rows)
    self_kaug, self_qaug, cross_kaug, cross_qaug, windows, prep_zero = call(
        prep_body, "prep",
        [((rows, TILE), BF16), ((MASK_ROWS, rows), BF16)] * 2 + [((4, rows // TILE), jnp.int32), ((1,), jnp.int32)],
        [tgt_lengths[0], tgt_pad, src_segments[0].reshape(-1, TILE), src_segments[0].reshape(-1, 1)],
        (0, 1), 2, out_smem=(4, 5),
    )
    if direct:
        self_block, cross_block, ffn_block = call(
            pack_body, "pack",
            [((1, 3 * BLOCK, width), BF16), ((1, 6 * BLOCK, width), BF16), ((parts * BLOCK + each, width), BF16)],
            [self_qkv, self_out, cross_qkv, cross_out, ffn_in, ffn_out, ln_gain, ln_bias], (), 1,
        )
        self_low, self_high = gather_blocks(self_block, devices, prep_zero[0])
        cross_held = cross_block
        for bit in reversed(range(2, bit_count(devices))):
            cross_held = jnp.concatenate([cross_held, exchange(cross_held, bit, devices)], axis=0)
        cross_came = exchange(cross_held, 1, devices)
        ffn_all = lax.all_gather(ffn_block, AXES, axis=0, tiled=False)
    else:
        inner_rows = jnp.concatenate([ffn_in[:, at * width : (at + 1) * width] for at in range(parts)], axis=0)
        cross_block = jnp.concatenate([cross_qkv.reshape(-1, width), cross_out, self_out], axis=0)
        self_low, self_high = gather_plain(self_qkv.reshape(-1, width), own, blocks)
        cross_low, cross_high = gather_plain(cross_block, own, blocks)
        scale_all = lax.all_gather(jnp.concatenate([ln_gain, ln_bias], axis=0), AXES, axis=1, tiled=True)
        scale_all = scale_all.reshape(-1, blocks, BLOCK).transpose(1, 0, 2)
        scale_all = jnp.pad(scale_all, ((0, 0), (0, BLOCK - scale_all.shape[1]), (0, width - BLOCK)))
        cross_low = jnp.concatenate([cross_low, scale_all[: blocks // 2]], axis=1)
        cross_high = jnp.concatenate([cross_high, scale_all[blocks // 2 :]], axis=1)
        inner_all = jnp.concatenate(gather_plain(inner_rows, own, blocks), axis=0)
        outer_all = jnp.concatenate(gather_plain(ffn_out, ffn_out.shape[0], blocks), axis=0)
        ffn_all = jnp.concatenate([inner_all, outer_all], axis=1)

    halves, halves_t, masses = (2, rows, width // 2), (2, width // 2, rows), (2, 8, rows)
    saved = [(halves, BF16), (halves_t, BF16), (halves, BF16), (halves_t, BF16), (halves, BF16), (halves_t, BF16), (masses, F32)]
    pipeline = [(halves_t, BF16), ((2, rows, 2 * TILE), F32), ((2, rows, 2 * TILE), BF16)]
    queries, queries_t, keys, keys_t, values, mixed_t, log_mass, weights, zero = call(
        self_forward_body, "self_forward", saved + [((3, width, width), BF16), ((1,), jnp.int32)],
        [self_low, self_high, token_rows, self_kaug, self_qaug, spots, windows],
        (5, 6), 15, pipeline, out_smem=(8,), near=(0, 1), limit=44,
    )
    if direct:
        cross_low = join(cross_held, cross_came, zero[0])
        cross_high = exchange(cross_low, 0, devices)
    (
        hidden_one, hidden_two, first_low, cross_queries, cross_queries_t, cross_keys, cross_keys_t, cross_values,
        cross_mixed_t, cross_mass, cross_weights, scales,
    ) = call(
        cross_forward_body, "cross_forward",
        [(square, F32)] * 2 + [(square, BF16)] + saved + [((5, width, width), BF16), ((BLOCK, width), F32)],
        [cross_low, cross_high, token_rows, mixed_t, encoder_rows, cross_kaug, cross_qaug, spots, windows],
        (7, 8), 18, pipeline + [(square, F32)], near=(0, 1), limit=50,
    )
    inside = parts * BLOCK + BLOCK
    most = inside + each
    result, grad_two, scale_grads, ffn_grads = call(
        feed_forward_body, "feed_forward",
        [(square, BF16), (square, F32), ((8, width), F32), ((blocks, most, width), BF16)],
        [ffn_all, hidden_two, out_grad[0], scales, cross_mixed_t, spots],
        (5,), 30,
        [
            ((width, wide), BF16), ((wide, width), BF16), ((wide, width), BF16), ((width, wide), BF16),
            (square, BF16), ((rows, wide), BF16), ((256, wide), F32), (square, BF16), ((rows, wide), BF16), (square, BF16),
            ((8, 8, width), F32), ((blocks, most, width), BF16),
        ],
        by_part=(3,),
    )
    if direct:
        near_groups = [[8 * at + other for other in range(8)] for at in range(4)]
        far_groups = [[at + 8 * other for other in range(4)] for at in range(8)]
        ffn_sum = lax.psum_scatter(ffn_grads, AXES, scatter_dimension=0, axis_index_groups=near_groups, tiled=True)
        ffn_sum = lax.psum_scatter(ffn_sum, AXES, scatter_dimension=0, axis_index_groups=far_groups, tiled=True)
        ffn_sum = ffn_sum[0].astype(F32)
        ffn_in_grad = jnp.concatenate([ffn_sum[at * BLOCK : (at + 1) * BLOCK] for at in range(parts)], axis=1)
        cross_out_grad = ffn_sum[parts * BLOCK : inside]
        ffn_out_grad = ffn_sum[inside:]
    work = [(halves, BF16), (halves_t, BF16), (masses, F32), (halves_t, F32), (halves, F32), (halves, F32)]
    grad_one, self_branch, cross_key_low, cross_value_low, cross_keep, cross_send = call(
        cross_backward_body, "cross_backward",
        [(square, F32), (square, BF16)] + [(halves, BF16)] * 2 + [((blocks // 2, 5 * BLOCK, width), BF16)] * 2,
        [
            grad_two, (cross_weights, 3), cross_mixed_t, cross_queries_t, cross_keys, cross_kaug, cross_qaug, cross_values,
            cross_mass, cross_queries, cross_keys_t, (cross_weights, 0), scales, hidden_one, first_low, encoder_rows, mixed_t,
            scale_grads, windows, spots,
        ],
        (18, 19), 25,
        [(square, BF16), (halves, BF16)] + work + [((2, 8, width), F32), ((blocks, 5 * BLOCK, width), BF16)],
        by_part=(4, 5),
    )

    grid = (2, 2, 2, 2)
    if direct:
        cross_came = exchange(cross_send, 0, devices)
    query_low, key_low, value_low, self_keep, self_send = call(
        self_backward_body, "self_backward",
        [(halves, BF16)] * 3 + [((blocks // 2, 3 * BLOCK, width), BF16)] * 2,
        [
            self_branch, (cross_weights, 4), mixed_t, queries_t, keys, self_kaug, self_qaug, values, log_mass, queries, keys_t,
            token_rows, windows, spots,
        ],
        (12, 13), 25, work + [((blocks, 3 * BLOCK, width), BF16)], by_part=(3, 4),
    )
    after = ()
    if direct:

        def cube(value):
            return value.reshape(grid + value.shape[1:])

        self_came = exchange(self_send, 0, devices)
        ((cross_keep, cross_send),) = fold(
            "fold_cross", [([(cube(cross_keep), cube(cross_came), 0, 0)], 0)], (query_low,)
        )
        cross_came = exchange(cross_send, 1, devices)
        ((self_keep, self_send),) = fold("fold_self", [([(cube(self_keep), cube(self_came), 0, 0)], 1)], (cross_send,))
        self_came = exchange(self_send, 2, devices)
        after = (cross_send, self_send)
    (encoder_grad,) = call(
        encoder_grad_body, "encoder_grad", [(square, BF16)],
        [cross_key_low, cross_value_low, (cross_weights, slice(1, 3))], (), 4, after=after, limit=32,
    )
    if direct:
        (cross_keep, cross_send), (self_keep, self_send) = fold(
            "fold_second", [([(cross_keep, cross_came, 0, 0)], 0), ([(self_keep, self_came, 0, 0)], 0)], (encoder_grad,)
        )
        cross_came = exchange(cross_send, 2, devices)
        self_came = exchange(self_send, 1, devices)
        after = (cross_send, self_send)
    (tokens_grad,) = call(
        tokens_grad_body, "tokens_grad", [(square, BF16)], [grad_one, weights, query_low, key_low, value_low], (), 5,
        after=after, limit=32,
    )
    if direct:
        ((rest_keep, rest_send),) = fold(
            "fold_third", [([(cross_keep, cross_came, 0, 0), (self_keep, self_came, 5 * BLOCK, 0)], 0)], (tokens_grad,)
        )
        rest_came = exchange(rest_send, 3, devices)
        ((rest_keep, rest_send),) = fold("fold_fourth", [([(rest_keep, rest_came, 0, 0)], 0)])
        rest_came = exchange(rest_send, 4, devices)
        cross_qkv_grad, self_out_grad, gain_grad, offset_grad, self_qkv_grad = call_near(
            total_body, "total",
            [((3, own, width), F32), ((own, width), F32), ((3, own), F32), ((3, own), F32), ((3, own, width), F32)],
            [rest_keep, rest_came], 1,
        )
    else:

        def add_up(grads, first, last, per):
            piece = grads[:, first:last].reshape(blocks, -1, per, width).transpose(1, 0, 2, 3)
            piece = piece.reshape(piece.shape[0], blocks * per, width)
            return lax.psum_scatter(piece.astype(F32), AXES, scatter_dimension=1, tiled=True)

        cross_grads = jnp.concatenate([cross_keep, cross_send], axis=0)
        self_grads = jnp.concatenate([self_keep, self_send], axis=0)
        inner_sum = add_up(ffn_grads, 0, parts * BLOCK, BLOCK)
        ffn_in_grad = inner_sum.transpose(1, 0, 2).reshape(own, wide)
        ffn_out_grad = add_up(ffn_grads, inside, most, each)[0]
        cross_out_grad = add_up(ffn_grads, parts * BLOCK, inside, BLOCK)[0]
        cross_qkv_grad = add_up(cross_grads, 0, 3 * BLOCK, BLOCK)
        self_out_grad = add_up(cross_grads, 3 * BLOCK, 4 * BLOCK, BLOCK)[0]
        scale_parts = cross_grads[:, 4 * BLOCK : 4 * BLOCK + 6, :BLOCK].astype(F32)
        scale_parts = scale_parts.transpose(1, 0, 2).reshape(6, width)
        scale_sum = lax.psum_scatter(scale_parts, AXES, scatter_dimension=1, tiled=True)
        gain_grad, offset_grad = scale_sum[:3], scale_sum[3:]
        self_qkv_grad = add_up(self_grads, 0, 3 * BLOCK, BLOCK)
    return (
        result[None], tokens_grad[None], encoder_grad[None], self_qkv_grad, self_out_grad, cross_qkv_grad,
        cross_out_grad, ffn_in_grad, ffn_out_grad, gain_grad, offset_grad,
    )


def solution(mesh):
    rows, first, second = P(AXES, None, None), P(AXES, None), P(None, AXES, None)
    columns = P(None, AXES)
    in_specs = (
        rows, rows, rows, second, first, second, first, first, first, columns, columns, first, P(AXES), first,
    )
    out_specs = (rows, rows, rows, second, first, second, first, first, first, columns, columns)
    return jax.shard_map(local, mesh=mesh, in_specs=in_specs, out_specs=out_specs, check_vma=False)
```

profile of v0, /device:TPU:0, one launch (start us, length us, event | category | flops | bytes accessed | tf_op | source)
XLA Modules:
  0.0 244.6 jit_solution(8720010902093638025)
XLA Ops:
  7.2 1.8 pack.1
  9.1 4.1 %collective-permute-start.4 = (bf16[1,48,512]{2,1,0:T(8,128)(2,1)}, bf16[1,48,512]{2,1,0:T(8,128)(2,1)S(1)}, u32[]{:S(2)}, u32[]{:S(2)}) collective-permute-start(bf16[1,48,512]{2,1,0:T(8,128)(2,1)} %get-tuple-element.75), channel_id=1, source_target_pairs={{0,16},{1,17},{2,18},{3,19},{4,20},{5,21},{6,22},{7,23},{8,24},{9,... | collective-permute-start | bytes 147464 | tf_op jit(solution)/shard_map/across_zz/ppermute | solution.py:771
  13.3 1.0 copy.25.refs_3_
  15.0 4.9 %prep.1 = (bf16[1024,128]{1,0:T(8,128)(2,1)}, bf16[32,1024]{1,0:T(8,128)(2,1)}, bf16[1024,128]{1,0:T(8,128)(2,1)}, bf16[32,1024]{1,0:T(8,128)(2,1)}, s32[4,8]{1,0:T(4,128)}, /*index=5*/s32[1]{0:T(128)}) custom-call(s32[16]{0:T(128)} %bitcast.47, s32[1]{0:T(128)S(6)} %copy.36.refs_1_, s32[8,128]{1,0:T(8,128)} %bitcast.41, s32[1024,1]{1,0:T(8,128)} %copy.25.refs_3_), custom_call_target="tpu_custom_call" | custom-call | flops 2000000000 | tf_op jit(solution)/shard_map/prep/pallas_call | solution.py:108
  21.3 1.9 collective-permute-start.5
  23.2 3.1 %collective-permute-done.5 = bf16[2,48,512]{2,1,0:T(8,128)(2,1)S(1)} collective-permute-done((bf16[2,48,512]{2,1,0:T(8,128)(2,1)S(1)}, bf16[2,48,512]{2,1,0:T(8,128)(2,1)S(1)}, u32[]{:S(2)}, u32[]{:S(2)}) %collective-permute-start.5) | collective-permute-done | bytes 98336 | tf_op jit(solution)/shard_map/across_z/ppermute | solution.py:771
  26.3 2.1 collective-permute-start.6
  28.4 1.4 collective-permute-start.1
  29.8 2.2 collective-permute-done.6
  32.1 2.0 collective-permute-start.7
  34.2 0.9 collective-permute-done.1
  35.1 1.0 collective-permute-start.2
  36.1 4.1 %collective-permute-done.7 = bf16[8,48,512]{2,1,0:T(8,128)(2,1)S(1)} collective-permute-done((bf16[8,48,512]{2,1,0:T(8,128)(2,1)S(1)}, bf16[8,48,512]{2,1,0:T(8,128)(2,1)S(1)}, u32[]{:S(2)}, u32[]{:S(2)}) %collective-permute-start.7) | collective-permute-done | bytes 393248 | tf_op jit(solution)/shard_map/across_x/ppermute | solution.py:771
  40.5 4.7 %collective-permute-done.2 = bf16[4,96,512]{2,1,0:T(8,128)(2,1)S(1)} collective-permute-done((bf16[4,96,512]{2,1,0:T(8,128)(2,1)S(1)}, bf16[4,96,512]{2,1,0:T(8,128)(2,1)S(1)}, u32[]{:S(2)}, u32[]{:S(2)}) %collective-permute-start.2) | collective-permute-done | bytes 393248 | tf_op jit(solution)/shard_map/across_y/ppermute | solution.py:771
  45.4 1.1 collective-permute-start.3
  46.6 1.1 copy-done.34
  47.7 13.9 %self_forward.1 = (bf16[2,1024,256]{2,1,0:T(8,128)(2,1)S(1)}, bf16[2,256,1024]{2,1,0:T(8,128)(2,1)S(1)}, bf16[2,1024,256]{2,1,0:T(8,128)(2,1)S(1)}, bf16[2,256,1...) custom-call(bf16[16,48,512]{2,1,0:T(8,128)(2,1)S(1)} %constant_dynam, ...), custom_call_target="tpu_custom_call" | custom-call | flops 15000000512 | tf_op jit(solution)/shard_map/self_forward/pallas_call | solution.py:108
  61.7 1.0 copy-done.19
  62.7 1.0 copy-done.20
  63.6 1.0 copy-done.21
  64.6 1.0 copy-done.22
  65.6 1.0 copy-done.23
  66.6 1.0 copy-done.24
  67.5 0.6 copy-done.29
  69.5 1.0 constant_dynamic-update-slice_fusion.8.refs_0_
  70.5 3.7 %collective-permute-done.9.refs_1_ = bf16[16,96,512]{2,1,0:T(8,128)(2,1)S(1)} collective-permute-done((bf16[16,96,512]{2,1,0:T(8,128)(2,1)}, bf16[16,96,512]{2,1,0:T(8,128)(2,1)S(1)}, u32[]{:S(2)}, u32[]{:S(2)}) %collective-permute-start.9) | collective-permute-done | bytes 1572896 | tf_op jit(solution)/shard_map/across_core/ppermute | solution.py:771
  74.2 1.1 copy-done.36
  75.3 19.9 %cross_forward.1 = (f32[1024,512]{1,0:T(8,128)}, f32[1024,512]{1,0:T(8,128)}, bf16[1024,512]{1,0:T(8,128)(2,1)S(1)}, bf16[2,1024,256]{2,1,0:T(8,128)(2,1)S(1)}, ...) custom-call(bf16[16,96,512]{2,1,0:T(8,128)(2,1)} %constant_dynamic-u, ...), custom_call_target="tpu_custom_call" | custom-call | flops 17999998976 | tf_op jit(solution)/shard_map/cross_forward/pallas_call | solution.py:108
  95.2 1.0 copy-done.25
  96.2 1.0 copy-done.26
  97.2 1.0 copy-done.27
  98.2 0.6 copy-done.30
  98.8 0.6 copy-done.31
  99.4 26.9 %feed_forward.1 = (bf16[1024,512]{1,0:T(8,128)(2,1)}, f32[1024,512]{1,0:T(8,128)}, f32[8,512]{1,0:T(8,128)}, bf16[32,144,512]{2,1,0:T(8,128)(2,1)}) custom-call(bf16[32,128,512]{2,1,0:T(8,128)(2,1)} %bitcast.43, f32[1024,512]{1,0:T(8,128)} %get-tuple-element.84.refs_1_, bf16[1024,512]{1,0:T(8,128)(2,1)} %bitcast.44, f32[16,512]{1,0:T(8,128)} %copy-done.31, ...), custom_call_target="tpu_custom_call" | custom-call | flops 30000001024 | tf_op jit(solution)/shard_map/feed_forward/pallas_call | solution.py:108
  126.3 22.5 %cross_backward.1 = (f32[1024,512]{1,0:T(8,128)}, bf16[1024,512]{1,0:T(8,128)(2,1)}, bf16[2,1024,256]{2,1,0:T(8,128)(2,1)}, bf16[2,1024,256]{2,1,0:T(8,128)(2,1)...) custom-call(f32[1024,512]{1,0:T(8,128)} %get-tuple-element.88.refs_0_, ...), custom_call_target="tpu_custom_call" | custom-call | flops 24999999488 | tf_op jit(solution)/shard_map/cross_backward/pallas_call | solution.py:108
  148.9 1.6 collective-permute-start.10
  150.5 23.9 %self_backward.1 = (bf16[2,1024,256]{2,1,0:T(8,128)(2,1)}, bf16[2,1024,256]{2,1,0:T(8,128)(2,1)}, bf16[2,1024,256]{2,1,0:T(8,128)(2,1)}, bf16[16,48,512]{2,1,0:T(8,128)(2,1)}, bf16[16,48,512]{2,1,0:T(8,128)(2,1)}) custom-call(bf16[1024,512]{1,0:T(8,128)(2,1)} %get-tuple-element.101.refs_0_, bf16[5,512,512]{2,1,0:T(8,128)(2,1)} %get-tuple-element.89.refs_1_.refs_11_.refs_2_, ...), custom_call_target="tpu_custom_call" | custom-call | flops 24999999488 | tf_op jit(solution)/shard_map/self_backward/pallas_call | solution.py:108
  174.4 0.9 collective-permute-start.12
  175.4 1.2 copy-done.6
  177.0 0.4 collective-permute-done.12
  177.9 0.8 collective-permute-start.13
  178.8 0.7 copy-done.8
  179.7 0.3 copy-done.11
  180.1 3.1 %encoder_grad.1.refs_4_ = bf16[1024,512]{1,0:T(8,128)(2,1)} custom-call(bf16[2,1024,256]{2,1,0:T(8,128)(2,1)S(1)} %copy-done.10, bf16[2,1024,256]{2,1,0:T(8,128)(2,1)S(1)} %copy-done.11, bf16[5,512,512]{2,1,0:T(8,128)(2,1)S(1)} %copy-done.8, bf16[2,2,2,80,512]{4,3,2,1,0:T(8,128)(2,1)S(1)} %get-tuple-element.114.refs_2_.refs_3_, ...), custom_call_target="tpu_custom_call" | custom-call | flops 4000000000 | tf_op jit(solution)/shard_map/encoder_grad/pallas_call | solution.py:108
  183.2 9.0 %collective-permute-done.13.refs_3_ = bf16[2,2,2,48,512]{4,3,2,1,0:T(8,128)(2,1)S(1)} collective-permute-done((bf16[2,2,2,48,512]{4,3,2,1,0:T(8,128)(2,1)S(1)}, bf16[2,2,2,48,512]{4,3,2,1,0:T(8,128)(2,1)S(1)}, u32[]{:S(2)}, u32[]{:S(2)}) %collective-permute-start.13) | collective-permute-done | bytes 393248 | tf_op jit(solution)/shard_map/across_y/ppermute | solution.py:771
  192.1 5.6 %collective-permute-done.11.refs_1_ = bf16[2,2,2,80,512]{4,3,2,1,0:T(8,128)(2,1)S(1)} collective-permute-done((bf16[2,2,2,80,512]{4,3,2,1,0:T(8,128)(2,1)S(1)}, bf16[2,2,2,80,512]{4,3,2,1,0:T(8,128)(2,1)S(1)}, u32[]{:S(2)}, u32[]{:S(2)}) %collective-permute-start.11) | collective-permute-done | bytes 655392 | tf_op jit(solution)/shard_map/across_x/ppermute | solution.py:771
  197.7 1.2 copy-done.3
  199.2 1.5 collective-permute-start.14
  200.7 0.6 collective-permute-start.15
  201.4 1.6 copy-done.9
  202.9 1.4 copy-done.12
  204.3 1.2 copy-done.13
  205.6 1.2 copy-done.14
  206.8 3.9 %tokens_grad.1.refs_4_ = bf16[1024,512]{1,0:T(8,128)(2,1)} custom-call(f32[1024,512]{1,0:T(8,128)S(1)} %copy-done.9, bf16[3,512,512]{2,1,0:T(8,128)(2,1)S(1)} %copy-done.12, bf16[2,1024,256]{2,1,0:T(8,128)(2,1)S(1)} %copy-done.7, bf16[2,1024,256]{2,1,0:T(8,128)(2,1)S(1)} %copy-done.13, bf16[2,1024,256]{2,1,0:T(8,128)(2,1)S(1)} %copy-done.14, ...), custom_call_target="tpu_custom_call" | custom-call | flops 5000000000 | tf_op jit(solution)/shard_map/tokens_grad/pallas_call | solution.py:108
  210.7 1.2 copy-done.4
  212.1 1.6 collective-permute-start.16
  213.6 11.4 %collective-permute-done.16.refs_1_ = bf16[2,128,512]{2,1,0:T(8,128)(2,1)S(1)} collective-permute-done((bf16[2,128,512]{2,1,0:T(8,128)(2,1)S(1)}, bf16[2,128,512]{2,1,0:T(8,128)(2,1)S(1)}, u32[]{:S(2)}, u32[]{:S(2)}) %collective-permute-start.16) | collective-permute-done | bytes 262176 | tf_op jit(solution)/shard_map/across_z/ppermute | solution.py:771
  225.1 2.0 collective-permute-start.17
  227.1 7.2 %collective-permute-done.17.refs_1_ = bf16[128,512]{1,0:T(8,128)(2,1)S(1)} collective-permute-done((bf16[128,512]{1,0:T(8,128)(2,1)S(1)}, bf16[128,512]{1,0:T(8,128)(2,1)S(1)}, u32[]{:S(2)}, u32[]{:S(2)}) %collective-permute-start.17) | collective-permute-done | bytes 131104 | tf_op jit(solution)/shard_map/across_zz/ppermute | solution.py:771
  234.3 0.7 total.1
  235.0 0.9 convert_element_type.4
  235.9 0.6 slice_bitcast_fusion.4
  236.6 0.7 slice_bitcast_fusion
  237.2 0.7 pad_maximum_fusion.5
  (94 shorter events, 2.5 us)
Async XLA Ops:
  7.2 6.1 %copy-start.35 = (s32[1,1024]{1,0:T(1,128)S(1)}, s32[1,1024]{1,0:T(1,128)}, u32[]{:S(2)}) copy-start(s32[1,1024]{1,0:T(1,128)} %param.27) | copy-start | bytes 12292
  7.2 92.2 %all-gather.3.cloned.1.call-start = ((), (), s32[]{:S(2)}) async-start(), calls=%async_computation.4 | async-start | bytes 4325376 | tf_op jit(solution)/shard_map/all_gather | solution.py:855
  9.0 192.3 %reduce-scatter.3.cloned.1.call-start = ((), (), s32[]{:S(2)}) async-start(), calls=%async_computation.2 | async-start | bytes 5308416 | tf_op jit(solution)/shard_map/reduce_scatter | solution.py:907
  9.1 12.1 %collective-permute-start.4 = (bf16[1,48,512]{2,1,0:T(8,128)(2,1)}, bf16[1,48,512]{2,1,0:T(8,128)(2,1)S(1)}, u32[]{:S(2)}, u32[]{:S(2)}) collective-permute-start(bf16[1,48,512]{2,1,0:T(8,128)(2,1)} %get-tuple-element.75), channel_id=1, source_target_pairs={{0,16},{1,17},{2,18},{3,19},{4,20},{5,21},{6,22},{7,23},{8,24},{9,... | collective-permute-start | bytes 147464 | tf_op jit(solution)/shard_map/across_zz/ppermute | solution.py:771
  13.2 15.2 %collective-permute-start = (bf16[1,96,512]{2,1,0:T(8,128)(2,1)}, bf16[1,96,512]{2,1,0:T(8,128)(2,1)S(1)}, u32[]{:S(2)}, u32[]{:S(2)}) collective-permute-start(bf16[1,96,512]{2,1,0:T(8,128)(2,1)} %get-tuple-element.74), channel_id=1, source_target_pairs={{0,16},{1,17},{2,18},{3,19},{4,20},{5,21},{6,22},{7,23},{8,24},{9,... | collective-permute-start | bytes 294920 | tf_op jit(solution)/shard_map/across_zz/ppermute | solution.py:771
  14.9 6.3 %copy-start.33 = (bf16[1,48,512]{2,1,0:T(8,128)(2,1)S(1)}, bf16[1,48,512]{2,1,0:T(8,128)(2,1)}, u32[]{:S(2)}) copy-start(bf16[1,48,512]{2,1,0:T(8,128)(2,1)} %get-tuple-element.75) | copy-start | bytes 147460
  15.0 13.4 %copy-start.32 = (bf16[1,96,512]{2,1,0:T(8,128)(2,1)S(1)}, bf16[1,96,512]{2,1,0:T(8,128)(2,1)}, u32[]{:S(2)}) copy-start(bf16[1,96,512]{2,1,0:T(8,128)(2,1)} %get-tuple-element.74) | copy-start | bytes 294916
  21.3 5.0 %collective-permute-start.5 = (bf16[2,48,512]{2,1,0:T(8,128)(2,1)S(1)}, bf16[2,48,512]{2,1,0:T(8,128)(2,1)S(1)}, u32[]{:S(2)}, u32[]{:S(2)}) collective-permute-start(bf16[2,48,512]{2,1,0:T(8,128)(2,1)S(1)} %pad_maximum_fusion.6), channel_id=1, source_target_pairs={{0,8},{1,9},{2,10},{3,11},{4,12},{5,13},{6,14},{7,15},{8,0},{9,1},... | collective-permute-start | bytes 294920 | tf_op jit(solution)/shard_map/across_z/ppermute | solution.py:771
  26.3 5.7 %collective-permute-start.6 = (bf16[4,48,512]{2,1,0:T(8,128)(2,1)S(1)}, bf16[4,48,512]{2,1,0:T(8,128)(2,1)S(1)}, u32[]{:S(2)}, u32[]{:S(2)}) collective-permute-start(bf16[4,48,512]{2,1,0:T(8,128)(2,1)S(1)} %pad_maximum_fusion.4), channel_id=1, source_target_pairs={{0,4},{1,5},{2,6},{3,7},{4,0},{5,1},{6,2},{7,3},{8,12},{9,13},{10,... | collective-permute-start | bytes 589832 | tf_op jit(solution)/shard_map/across_y/ppermute | solution.py:771
  28.4 6.6 %collective-permute-start.1 = (bf16[2,96,512]{2,1,0:T(8,128)(2,1)S(1)}, bf16[2,96,512]{2,1,0:T(8,128)(2,1)S(1)}, u32[]{:S(2)}, u32[]{:S(2)}) collective-permute-start(bf16[2,96,512]{2,1,0:T(8,128)(2,1)S(1)} %pad_maximum_fusion.3), channel_id=1, source_target_pairs={{0,8},{1,9},{2,10},{3,11},{4,12},{5,13},{6,14},{7,15},{8,0},{9,1},... | collective-permute-start | bytes 589832 | tf_op jit(solution)/shard_map/across_z/ppermute | solution.py:771
  32.1 8.1 %collective-permute-start.7 = (bf16[8,48,512]{2,1,0:T(8,128)(2,1)S(1)}, bf16[8,48,512]{2,1,0:T(8,128)(2,1)S(1)}, u32[]{:S(2)}, u32[]{:S(2)}) collective-permute-start(bf16[8,48,512]{2,1,0:T(8,128)(2,1)S(1)} %pad_maximum_fusion.2), channel_id=1, source_target_pairs={{0,2},{1,3},{2,0},{3,1},{4,6},{5,7},{6,4},{7,5},{8,10},{9,11},{10,... | collective-permute-start | bytes 1179656 | tf_op jit(solution)/shard_map/across_x/ppermute | solution.py:771
  35.1 10.2 %collective-permute-start.2 = (bf16[4,96,512]{2,1,0:T(8,128)(2,1)S(1)}, bf16[4,96,512]{2,1,0:T(8,128)(2,1)S(1)}, u32[]{:S(2)}, u32[]{:S(2)}) collective-permute-start(bf16[4,96,512]{2,1,0:T(8,128)(2,1)S(1)} %pad_maximum_fusion.1), channel_id=1, source_target_pairs={{0,4},{1,5},{2,6},{3,7},{4,0},{5,1},{6,2},{7,3},{8,12},{9,13},{10,... | collective-permute-start | bytes 1179656 | tf_op jit(solution)/shard_map/across_y/ppermute | solution.py:771
  40.3 6.3 %collective-permute-start.8 = (bf16[16,48,512]{2,1,0:T(8,128)(2,1)S(1)}, bf16[16,48,512]{2,1,0:T(8,128)(2,1)S(1)}, u32[]{:S(2)}, u32[]{:S(2)}) collective-permute-start(bf16[16,48,512]{2,1,0:T(8,128)(2,1)S(1)} %constant_dynamic-update-slice_fusion.9.refs_0_), channel_id=1, source_target_pairs={{0,1},{1,0},{2,3},{3,2},{4,5},{5,4},{6,7},{7,6},{8,9},{9,8},{10,11... | collective-permute-start | bytes 2359304 | tf_op jit(solution)/shard_map/across_core/ppermute | solution.py:771
  40.4 33.7 %copy-start = (s32[3]{0:T(128)}, s32[3]{0:T(128)S(1)}, u32[]{:S(2)}) copy-start(s32[3]{0:T(128)S(1)} %pad_add_fusion.refs_5_.refs_7_.refs_19_.refs_13_) | copy-start | bytes 40
  40.5 7.2 %copy-start.1 = (bf16[1,1024,512]{2,1,0:T(8,128)(2,1)S(1)}, bf16[1,1024,512]{2,1,0:T(8,128)(2,1)}, u32[]{:S(2)}) copy-start(bf16[1,1024,512]{2,1,0:T(8,128)(2,1)} %param.14) | copy-start | bytes 3145732
  40.5 7.2 %copy-start.15 = (bf16[1024,128]{1,0:T(8,128)(2,1)S(1)}, bf16[1024,128]{1,0:T(8,128)(2,1)}, u32[]{:S(2)}) copy-start(bf16[1024,128]{1,0:T(8,128)(2,1)} %get-tuple-element.77.refs_3_.refs_5_) | copy-start | bytes 786436
  40.5 7.2 %copy-start.17 = (bf16[32,1024]{1,0:T(8,128)(2,1)S(1)}, bf16[32,1024]{1,0:T(8,128)(2,1)}, u32[]{:S(2)}) copy-start(bf16[32,1024]{1,0:T(8,128)(2,1)} %get-tuple-element.78.refs_4_.refs_6_) | copy-start | bytes 196612
  40.5 7.2 %copy-start.28 = (s32[4,8]{1,0:T(4,128)S(1)}, s32[4,8]{1,0:T(4,128)}, u32[]{:S(2)}) copy-start(s32[4,8]{1,0:T(4,128)} %get-tuple-element.79.refs_6_.refs_8_.refs_18_.refs_12_) | copy-start | bytes 388
  45.4 24.2 %collective-permute-start.3 = (bf16[8,96,512]{2,1,0:T(8,128)(2,1)S(1)}, bf16[8,96,512]{2,1,0:T(8,128)(2,1)S(1)}, u32[]{:S(2)}, u32[]{:S(2)}) collective-permute-start(bf16[8,96,512]{2,1,0:T(8,128)(2,1)S(1)} %pad_maximum_fusion), channel_id=1, source_target_pairs={{0,2},{1,3},{2,0},{3,1},{4,6},{5,7},{6,4},{7,5},{8,10},{9,11},{10,... | collective-permute-start | bytes 2359304 | tf_op jit(solution)/shard_map/across_x/ppermute | solution.py:771
  46.6 1.1 copy-start.34
  61.7 1.0 copy-start.19
  62.7 1.0 copy-start.20
  63.6 1.0 copy-start.21
  64.6 1.0 copy-start.22
  65.6 1.0 copy-start.23
  66.6 1.0 copy-start.24
  67.5 0.6 copy-start.29
  68.2 7.1 %copy-start.16 = (bf16[1024,128]{1,0:T(8,128)(2,1)S(1)}, bf16[1024,128]{1,0:T(8,128)(2,1)}, u32[]{:S(2)}) copy-start(bf16[1024,128]{1,0:T(8,128)(2,1)} %get-tuple-element.82.refs_5_) | copy-start | bytes 786436
  68.2 7.1 %copy-start.18 = (bf16[32,1024]{1,0:T(8,128)(2,1)S(1)}, bf16[32,1024]{1,0:T(8,128)(2,1)}, u32[]{:S(2)}) copy-start(bf16[32,1024]{1,0:T(8,128)(2,1)} %get-tuple-element.83.refs_6_) | copy-start | bytes 196612
  70.5 3.7 %collective-permute-start.9 = (bf16[16,96,512]{2,1,0:T(8,128)(2,1)}, bf16[16,96,512]{2,1,0:T(8,128)(2,1)S(1)}, u32[]{:S(2)}, u32[]{:S(2)}) collective-permute-start(bf16[16,96,512]{2,1,0:T(8,128)(2,1)} %constant_dynamic-update-slice_fusion.8.refs_0_), channel_id=1, source_target_pairs={{0,1},{1,0},{2,3},{3,2},{4,5},{5,4},{6,7},{7,6},{8,9},{9,8},{10,11... | collective-permute-start | bytes 4718600 | tf_op jit(solution)/shard_map/across_core/ppermute | solution.py:771
  74.2 1.1 copy-start.36
  95.2 1.0 copy-start.25
  96.2 1.0 copy-start.26
  97.2 1.0 copy-start.27
  98.1 0.6 copy-start.30
  98.8 0.6 copy-start.31
  126.3 108.7 %reduce-scatter.5.cloned.1.call-start = ((), (), s32[]{:S(2)}) async-start(), calls=%async_computation.3 | async-start | bytes 737280 | tf_op jit(solution)/shard_map/reduce_scatter | solution.py:908
  148.9 26.5 %collective-permute-start.10 = (bf16[16,80,512]{2,1,0:T(8,128)(2,1)}, bf16[16,80,512]{2,1,0:T(8,128)(2,1)S(1)}, u32[]{:S(2)}, u32[]{:S(2)}) collective-permute-start(bf16[16,80,512]{2,1,0:T(8,128)(2,1)} %get-tuple-element.112), channel_id=1, source_target_pairs={{0,1},{1,0},{2,3},{3,2},{4,5},{5,4},{6,7},{7,6},{8,9},{9,8},{10,11... | collective-permute-start | bytes 3932168 | tf_op jit(solution)/shard_map/across_core/ppermute | solution.py:771
  150.5 24.9 %copy-start.2 = (bf16[16,80,512]{2,1,0:T(8,128)(2,1)S(1)}, bf16[16,80,512]{2,1,0:T(8,128)(2,1)}, u32[]{:S(2)}) copy-start(bf16[16,80,512]{2,1,0:T(8,128)(2,1)} %get-tuple-element.111) | copy-start | bytes 3932164
  174.4 3.1 %collective-permute-start.12 = (bf16[16,48,512]{2,1,0:T(8,128)(2,1)}, bf16[16,48,512]{2,1,0:T(8,128)(2,1)S(1)}, u32[]{:S(2)}, u32[]{:S(2)}) collective-permute-start(bf16[16,48,512]{2,1,0:T(8,128)(2,1)} %get-tuple-element.116), channel_id=1, source_target_pairs={{0,1},{1,0},{2,3},{3,2},{4,5},{5,4},{6,7},{7,6},{8,9},{9,8},{10,11... | collective-permute-start | bytes 2359304 | tf_op jit(solution)/shard_map/across_core/ppermute | solution.py:771
  175.4 1.2 copy-start.6
  176.6 1.1 copy-start.5
  176.9 20.8 %collective-permute-start.11 = (bf16[2,2,2,80,512]{4,3,2,1,0:T(8,128)(2,1)S(1)}, bf16[2,2,2,80,512]{4,3,2,1,0:T(8,128)(2,1)S(1)}, u32[]{:S(2)}, u32[]{:S(2)}) collective-permute-start(bf16[2,2,2,80,512]{4,3,2,1,0:T(8,128)(2,1)S(1)} %get-tuple-element.114.refs_2_.refs_3_), channel_id=1, source_target_pairs={{0,2},{1,3},{2,0},{3,1},{4,6},{5,7},{6,4},{7,5},{8,10},{9,11},{10,... | collective-permute-start | bytes 1966088 | tf_op jit(solution)/shard_map/across_x/ppermute | solution.py:771
  177.7 1.7 copy-start.8
  177.7 2.0 copy-start.10
  177.7 2.3 copy-start.11
  177.9 14.2 %collective-permute-start.13 = (bf16[2,2,2,48,512]{4,3,2,1,0:T(8,128)(2,1)S(1)}, bf16[2,2,2,48,512]{4,3,2,1,0:T(8,128)(2,1)S(1)}, u32[]{:S(2)}, u32[]{:S(2)}) collective-permute-start(bf16[2,2,2,48,512]{4,3,2,1,0:T(8,128)(2,1)S(1)} %get-tuple-element.118.refs_4_), channel_id=1, source_target_pairs={{0,4},{1,5},{2,6},{3,7},{4,0},{5,1},{6,2},{7,3},{8,12},{9,13},{10,... | collective-permute-start | bytes 1179656 | tf_op jit(solution)/shard_map/across_y/ppermute | solution.py:771
  197.7 1.2 copy-start.3
  199.0 2.4 copy-start.7
  199.2 11.5 %collective-permute-start.14 = (bf16[2,2,80,512]{3,2,1,0:T(8,128)(2,1)S(1)}, bf16[2,2,80,512]{3,2,1,0:T(8,128)(2,1)S(1)}, u32[]{:S(2)}, u32[]{:S(2)}) collective-permute-start(bf16[2,2,80,512]{3,2,1,0:T(8,128)(2,1)S(1)} %get-tuple-element.121.refs_5_), channel_id=1, source_target_pairs={{0,4},{1,5},{2,6},{3,7},{4,0},{5,1},{6,2},{7,3},{8,12},{9,13},{10,... | collective-permute-start | bytes 983048 | tf_op jit(solution)/shard_map/across_y/ppermute | solution.py:771
  200.7 10.0 %collective-permute-start.15 = (bf16[2,2,48,512]{3,2,1,0:T(8,128)(2,1)S(1)}, bf16[2,2,48,512]{3,2,1,0:T(8,128)(2,1)S(1)}, u32[]{:S(2)}, u32[]{:S(2)}) collective-permute-start(bf16[2,2,48,512]{3,2,1,0:T(8,128)(2,1)S(1)} %get-tuple-element.122.refs_6_), channel_id=1, source_target_pairs={{0,2},{1,3},{2,0},{3,1},{4,6},{5,7},{6,4},{7,5},{8,10},{9,11},{10,... | collective-permute-start | bytes 589832 | tf_op jit(solution)/shard_map/across_x/ppermute | solution.py:771
  201.3 1.6 copy-start.9
  202.9 1.4 copy-start.12
  204.3 1.2 copy-start.13
  205.6 1.2 copy-start.14
  210.7 1.2 copy-start.4
  212.1 12.9 %collective-permute-start.16 = (bf16[2,128,512]{2,1,0:T(8,128)(2,1)S(1)}, bf16[2,128,512]{2,1,0:T(8,128)(2,1)S(1)}, u32[]{:S(2)}, u32[]{:S(2)}) collective-permute-start(bf16[2,128,512]{2,1,0:T(8,128)(2,1)S(1)} %get-tuple-element.126), channel_id=1, source_target_pairs={{0,8},{1,9},{2,10},{3,11},{4,12},{5,13},{6,14},{7,15},{8,0},{9,1},... | collective-permute-start | bytes 786440 | tf_op jit(solution)/shard_map/across_z/ppermute | solution.py:771
  225.1 9.2 %collective-permute-start.17 = (bf16[128,512]{1,0:T(8,128)(2,1)S(1)}, bf16[128,512]{1,0:T(8,128)(2,1)S(1)}, u32[]{:S(2)}, u32[]{:S(2)}) collective-permute-start(bf16[128,512]{1,0:T(8,128)(2,1)S(1)} %get-tuple-element.128), channel_id=1, source_target_pairs={{0,16},{1,17},{2,18},{3,19},{4,20},{5,21},{6,22},{7,23},{8,24},{9,... | collective-permute-start | bytes 393224 | tf_op jit(solution)/shard_map/across_zz/ppermute | solution.py:771
Sparse Core Ops, SparseCore 0:
  11.5 70.1 all-gather.2
  126.4 62.4 reduce-scatter.2
  201.5 24.9 reduce-scatter.4
where the time goes:
time: 249 us; the launch traced here: 245 us
  Pallas kernels  122 us (49%)
  waiting for transfers between devices  52.4 us (21%)
  local copies, waits for them, and re-layouts  27.2 us (11%)
  starting transfers between devices  23.1 us (9%)
  between operations  17.6 us (7%)
    pallas_call x9, Pallas kernels, call(): pl.pallas_call(ordered, name=name, out_shape=[jax.ShapeDtypeStruct(shape,...  121 us
    ppermute x18, waiting for transfers between devices, exchange_bit(): lax.ppermute(value, AXES, [(at, at ^ 1 << bit) for at in range(devices)])  52.3 us
    unnamed x82, local copies, waits for them, and re-layouts  23.8 us
    ppermute x18, starting transfers between devices, exchange_bit(): lax.ppermute(value, AXES, [(at, at ^ 1 << bit) for at in range(devices)])  23 us
  transfers between devices with their start and end apart: 21, of which 11 were waited for; matrix products, arithmetic and copies ran while one was open for 1% of the time, Pallas kernels for 38%

commit v1 on v0

--- a/solution.py
+++ b/solution.py
@@ -65,11 +65,12 @@
 
     def need(self, *refs):
         for ref in refs:
-            self.coming.pop(id(ref)).wait()
+            if id(ref) in self.coming:
+                self.coming.pop(id(ref)).wait()
 
     def push(self, *refs):
         for ref in refs:
-            self.started.append(self.start(ref, self.going.pop(id(ref))))
+            self.started.append(self.start(*self.going.pop(id(ref))))
 
     def push_part(self, source, target):
         self.started.append(self.start(source, target))
@@ -77,21 +78,24 @@
     def finish(self):
         for copy in self.coming.values():
             copy.wait()
+        for ref, target in self.going.values():
+            self.started.append(self.start(ref, target))
         for copy in self.started:
             copy.wait()
 
 
-def call(body, name, outs, ins, in_smem, micros, scratch=(), out_smem=(), after=(), by_part=(), near=(), limit=58):
+def call(body, name, outs, ins, in_smem, micros, scratch=(), out_smem=(), after=(), by_part=(), stay=(), near=(), through=(), limit=48):
     ins = [one if isinstance(one, tuple) else (one, None) for one in ins]
     indexes = [index for _, index in ins]
     ins = [array for array, _ in ins]
     in_count, out_count = len(ins), len(outs)
     moved_in = [at for at in range(in_count) if at not in in_smem and at not in near]
-    moved_out = [at for at in range(out_count) if at not in out_smem and at not in by_part]
+    moved_out = [at for at in range(out_count) if at not in out_smem and at not in by_part and at not in stay]
+    ins = [pltpu.with_memory_space_constraint(one, pltpu.HBM) if at in moved_in else one for at, one in enumerate(ins)]
 
     def ordered(*refs):
-        sources, refs = list(refs[:in_count]), refs[in_count + len(after) :]
-        targets, refs = list(refs[:out_count]), refs[out_count:]
+        sources, refs = list(refs[:in_count]), refs[in_count + len(after) + len(through) :]
+        targets, refs = list(refs[:out_count]), refs[out_count + len(through) :]
         buffers_in, refs = refs[: len(moved_in)], refs[len(moved_in) :]
         buffers_out, refs = refs[: len(moved_out)], refs[len(moved_out) :]
         copies = Copies(refs[0])
@@ -100,7 +104,7 @@
             copies.coming[id(buffer)] = copies.start(source, buffer)
             sources[at] = buffer
         for at, buffer in zip(moved_out, buffers_out):
-            copies.going[id(buffer)] = targets[at]
+            copies.going[id(buffer)] = (buffer, targets[at])
             targets[at] = buffer
         body(copies, *sources, *targets, *refs[1:])
         copies.finish()
@@ -108,34 +112,44 @@
     return pl.pallas_call(
         ordered,
         name=name,
-        out_shape=[jax.ShapeDtypeStruct(shape, kind) for shape, kind in outs],
-        in_specs=[SMEM if at in in_smem else VMEM if at in near else HBM for at in range(in_count)] + [ANYWHERE] * len(after),
-        out_specs=[SMEM if at in out_smem else HBM for at in range(out_count)],
+        out_shape=[
+            jax.ShapeDtypeStruct(shape, kind) if at in out_smem else (pltpu.VMEM if at in stay else pltpu.HBM)(shape, kind)
+            for at, (shape, kind) in enumerate(outs)
+        ]
+        + [jax.ShapeDtypeStruct(one.shape, one.dtype) for one in through],
+        in_specs=[SMEM if at in in_smem else VMEM if at in near else HBM for at in range(in_count)]
+        + [ANYWHERE] * (len(after) + len(through)),
+        out_specs=[SMEM if at in out_smem else VMEM if at in stay else HBM for at in range(out_count)]
+        + [ANYWHERE] * len(through),
+        input_output_aliases={in_count + len(after) + at: out_count + at for at in range(len(through))},
         scratch_shapes=[pltpu.VMEM(part_shape(ins[at].shape, indexes[at]), ins[at].dtype) for at in moved_in]
         + [pltpu.VMEM(*outs[at]) for at in moved_out]
-        + [pltpu.SemaphoreType.DMA((len(moved_in) + len(moved_out) + 4 * len(by_part),))]
+        + [pltpu.SemaphoreType.DMA((len(moved_in) + len(moved_out) + 4 * len(by_part) + len(stay) + 1,))]
         + [pltpu.VMEM(shape, kind) for shape, kind in scratch],
         compiler_params=pltpu.CompilerParams(vmem_limit_bytes=limit * 2**20),
         cost_estimate=pl.CostEstimate(flops=int(micros * 1e9), bytes_accessed=0, transcendentals=0),
-    )(*ins, *after)
-
-
-def call_near(body, name, outs, ins, micros, after=()):
-    count = len(ins)
-    return pl.pallas_call(
-        lambda *refs: body(*refs[:count], *refs[count + len(after) :]),
+    )(*ins, *after, *through)
+
+
+def call_near(body, name, outs, ins, micros, after=(), through=(), stay=True):
+    count, skipped = len(ins), len(ins) + len(after) + len(through)
+    after = [pltpu.with_memory_space_constraint(one, pltpu.HBM) for one in after]
+    results = pl.pallas_call(
+        lambda *refs: body(*refs[:count], *refs[skipped : skipped + len(outs)]),
         name=name,
-        out_shape=[jax.ShapeDtypeStruct(shape, kind) for shape, kind in outs],
-        in_specs=[VMEM] * count + [ANYWHERE] * len(after),
-        out_specs=[VMEM] * len(outs),
+        out_shape=[pltpu.VMEM(shape, kind) if stay else jax.ShapeDtypeStruct(shape, kind) for shape, kind in outs]
+        + [jax.ShapeDtypeStruct(one.shape, one.dtype) for one in through],
+        in_specs=[VMEM] * count + [HBM] * len(after) + [ANYWHERE] * len(through),
+        out_specs=[VMEM] * len(outs) + [ANYWHERE] * len(through),
+        input_output_aliases={count + len(after) + at: len(outs) + at for at in range(len(through))},
         compiler_params=pltpu.CompilerParams(vmem_limit_bytes=16 * 2**20),
         cost_estimate=pl.CostEstimate(flops=int(micros * 1e9), bytes_accessed=0, transcendentals=0),
-    )(*ins, *after)
-
-
-def prep_body(copies, lengths, padding, src_grid, src_column, self_kaug, self_qaug, cross_kaug, cross_qaug, windows, zero):
-    zero[0] = 0
-    copies.need(src_grid, src_column)
+    )(*ins, *after, *through)
+    return results[: len(outs)], results[len(outs) :]
+
+
+def prep_body(copies, lengths, padding, src_grid, self_kaug, self_qaug, cross_kaug, cross_qaug, windows):
+    copies.need(src_grid)
     rows = self_kaug.shape[0]
     count = lengths.shape[0]
     edge = rows - padding[0]
@@ -158,7 +172,9 @@
         part = slice(tile * TILE, (tile + 1) * TILE)
         column_ids = labels(iota((TILE, TILE), 0) + tile * TILE)
         self_kaug[part, :] = jnp.where(column_ids == lanes, MASKED, ones_lanes).astype(BF16)
-        cross_kaug[part, :] = jnp.where(src_column[part, :] == lanes, MASKED, ones_lanes).astype(BF16)
+        source_row = src_grid[tile : tile + 1, :].astype(F32)
+        source_column = jnp.broadcast_to(source_row, (TILE, TILE)).T
+        cross_kaug[part, :] = jnp.where(source_column == lanes.astype(F32), MASKED, ones_lanes).astype(BF16)
     copies.push(self_kaug, self_qaug, cross_kaug, cross_qaug)
     for tile in range(rows // TILE):
         first, last = tile * TILE, tile * TILE + TILE - 1
@@ -371,20 +387,22 @@
     return sum(((number >> bit) & 1) << (4 - bit) for bit in range(5))
 
 
-def origin(spots, spot):
-    return jnp.where(spots[0] == 1, mirrored(spot) ^ spots[1], spot)
+def origin(spots, spot, swapped=False):
+    number = mirrored(spot)
+    if swapped:
+        number = (number & 25) | ((number & 2) << 1) | ((number & 4) >> 1)
+    return jnp.where(spots[0] == 1, number ^ spots[1], spot)
 
 
 def place(spots, block):
     return jnp.where(spots[0] == 1, mirrored(block) ^ spots[2], block)
 
 
-def take_blocks(spots, low, high, row, target):
-    half = low.shape[0]
-    for spot in range(2 * half):
-        source = low if spot < half else high
-        start = pl.multiple_of(origin(spots, spot) * BLOCK, BLOCK)
-        target[pl.ds(start, BLOCK), :] = source[spot % half, row : row + BLOCK, :]
+def take_blocks(spots, pieces, row, target, swapped=False):
+    each = pieces[0].shape[0]
+    for spot in range(each * len(pieces)):
+        start = pl.multiple_of(origin(spots, spot, swapped) * BLOCK, BLOCK)
+        target[pl.ds(start, BLOCK), :] = pieces[spot // each][spot % each, row : row + BLOCK, :]
 
 
 def put_blocks(spots, grads, first, rows_each, row, value):
@@ -437,13 +455,14 @@
 
 
 def self_forward_body(
-    copies, low, high, tokens, kaug, qaug, spots, windows,
-    queries, queries_t, keys, keys_t, values, mixed_t, log_mass, weights, zero,
+    copies, piece_one, piece_two, piece_three, piece_four, tokens, kaug, qaug, spots, windows,
+    queries, queries_t, keys, keys_t, values, mixed_t, log_mass, weights,
     values_t, scores, raised,
 ):
-    zero[0] = 0
+    pieces = (piece_one, piece_two, piece_three, piece_four)
+    copies.need(*pieces)
     for which in range(3):
-        take_blocks(spots, low, high, which * BLOCK, weights.at[which])
+        take_blocks(spots, pieces, which * BLOCK, weights.at[which])
     copies.push(weights)
     copies.need(tokens)
 
@@ -467,18 +486,23 @@
 
 
 def cross_forward_body(
-    copies, low, high, tokens, self_mixed_t, encoder, kaug, qaug, spots, windows,
+    copies, upper_one, upper_two, upper_three, upper_four, lower_one, lower_two, lower_three, lower_four,
+    tokens, self_mixed_t, encoder, kaug, qaug, spots, windows,
     hidden, hidden_two, first_low, queries, queries_t, keys, keys_t, values, mixed_t, log_mass, weights, scales,
     values_t, scores, raised, first,
 ):
-    for which in range(5):
-        take_blocks(spots, low, high, which * BLOCK, weights.at[which])
-    half = low.shape[0]
+    upper = (upper_one, upper_two, upper_three, upper_four)
+    lower = (lower_one, lower_two, lower_three, lower_four)
+    copies.need(*upper, *lower)
+    for which in range(3):
+        take_blocks(spots, upper, which * BLOCK, weights.at[which])
+    for which in range(2):
+        take_blocks(spots, lower, which * BLOCK, weights.at[3 + which], True)
+    each = lower_one.shape[0]
     gathered = jnp.zeros(scales.shape, F32)
-    for spot in range(2 * half):
-        source = low if spot < half else high
-        block = source[spot % half, 5 * BLOCK : 6 * BLOCK, :].astype(F32)
-        gathered = gathered + pltpu.roll(block, origin(spots, spot) * BLOCK, 1)
+    for spot in range(4 * each):
+        block = lower[spot // each][spot % each, 2 * BLOCK : 3 * BLOCK, :].astype(F32)
+        gathered = gathered + pltpu.roll(block, origin(spots, spot, True) * BLOCK, 1)
     scales[...] = gathered
     copies.push(weights, scales)
     gain, offset = scales[0:1, :], scales[3:4, :]
@@ -518,8 +542,8 @@
 
 def feed_forward_body(
     copies, gathered, hidden, out_grad, scales, cross_mixed_t, spots,
-    out, grad_two, scale_grads, weight_grads,
-    inner, outer, inner_t, outer_t, second_low, active, slope, branch, grad_inner, cross_branch, sums, grads,
+    out, grad_two, scale_grads, inner_grads, keep, send,
+    inner, outer, inner_t, outer_t, second_low, active, slope, branch, grad_inner, cross_branch, sums, grads, grads_out,
 ):
     rows, width = hidden.shape
     wide = outer.shape[0]
@@ -575,25 +599,26 @@
     copies.push(out, grad_two, scale_grads)
     inside = parts * BLOCK
 
-    def put(first, rows_each, row, value):
-        for at in range(value.shape[0] // rows_each):
+    def put(first, row, value):
+        for at in range(value.shape[0] // BLOCK):
             block = first + at
             spot = jnp.where(spots[0] == 1, (block % 8) * 4 + block // 8, block)
-            grads[spot, row : row + rows_each, :] = value[at * rows_each : (at + 1) * rows_each]
+            grads[spot, row : row + BLOCK, :] = value[at * BLOCK : (at + 1) * BLOCK]
 
     for at in range(parts):
         span = slice(at * width, (at + 1) * width)
-        put(at * width // each, each, inside + BLOCK, dot_tn(active[:, span], branch[...]).astype(BF16))
-    for at in range(parts):
-        span = slice(at * width, (at + 1) * width)
-        put(0, BLOCK, at * BLOCK, dot_tn(second_low[...], grad_inner[:, span]).astype(BF16))
-    copies.push_part(grads.at[:, 0:inside, :], weight_grads.at[:, 0:inside, :])
-    copies.push_part(grads.at[:, inside + BLOCK :, :], weight_grads.at[:, inside + BLOCK :, :])
+        put(0, at * BLOCK, dot_tn(second_low[...], grad_inner[:, span]).astype(BF16))
+    copies.push_part(grads.at[:, 0:inside, :], inner_grads.at[:, 0:inside, :])
     copies.need(cross_mixed_t)
     half_width = cross_mixed_t.shape[1]
     for half in range(cross_mixed_t.shape[0]):
-        put(half * half_width // BLOCK, BLOCK, inside, dot(cross_mixed_t[half], cross_branch[...]).astype(BF16))
-    copies.push_part(grads.at[:, inside : inside + BLOCK, :], weight_grads.at[:, inside : inside + BLOCK, :])
+        put(half * half_width // BLOCK, inside, dot(cross_mixed_t[half], cross_branch[...]).astype(BF16))
+    copies.push_part(grads.at[:, inside : inside + BLOCK, :], inner_grads.at[:, inside : inside + BLOCK, :])
+    for at in range(parts):
+        span = slice(at * width, (at + 1) * width)
+        value = dot_tn(active[:, span], branch[...]).astype(BF16)
+        put_blocks(spots, grads_out, at * width // each, each, 0, value)
+    hand_out(copies, grads_out, keep, send)
 
 
 def back_projections(grad_rows, weight, grad, grad_t):
@@ -731,13 +756,14 @@
     copies.push(tokens_grad)
 
 
-def fold_body(groups, *refs):
+def fold_body(groups, copies, *refs):
     count = sum(2 * len(terms) for terms, _ in groups)
     terms_refs, results = list(refs[:count]), list(refs[count:])
     for terms, axis in groups:
         keep, send = results.pop(0), results.pop(0)
         for row, column in terms:
             kept, came = terms_refs.pop(0), terms_refs.pop(0)
+            copies.need(kept)
             lead, (high, wide) = kept.shape[:-2], kept.shape[-2:]
             for number in range(math.prod(lead)):
                 index, left = [], number
@@ -749,7 +775,27 @@
                 target[(*index, slice(row, row + high), slice(column, column + wide))] = value
 
 
-def total_body(keep, came, cross_qkv, self_out, gain, offset, self_qkv):
+def order_body(copies, total, spots, keep, send):
+    copies.need(total)
+    near, far = (spots[1] >> 3) & 1, (spots[1] >> 4) & 1
+    for block in range(2):
+        keep[block] = total[near + 2 * (far ^ block)]
+        send[block] = total[(1 - near) + 2 * (far ^ block)]
+
+
+def inner_total_body(keep, came, ffn_in, cross_out):
+    width = cross_out.shape[1]
+    parts = ffn_in.shape[1] // width
+
+    def total(first):
+        return keep[first : first + BLOCK, :].astype(F32) + came[first : first + BLOCK, :].astype(F32)
+
+    for part in range(parts):
+        ffn_in[:, part * width : (part + 1) * width] = total(part * BLOCK)
+    cross_out[...] = total(parts * BLOCK)
+
+
+def total_body(keep, came, cross_qkv, self_out, gain, offset, self_qkv, ffn_out):
     def total(first, rows):
         return keep[first : first + rows, :].astype(F32) + came[first : first + rows, :].astype(F32)
 
@@ -757,6 +803,7 @@
         cross_qkv[which] = total(which * BLOCK, BLOCK)
         self_qkv[which] = total((5 + which) * BLOCK, BLOCK)
     self_out[...] = total(3 * BLOCK, BLOCK)
+    ffn_out[...] = total(8 * BLOCK, ffn_out.shape[0])
     scales = total(4 * BLOCK, BLOCK)
     gain[...] = scales[0:3, : gain.shape[1]]
     offset[...] = scales[3:6, : offset.shape[1]]
@@ -775,17 +822,44 @@
     return devices.bit_length() - 1
 
 
-def join(first, second, zero):
-    both = jnp.concatenate([first, jnp.zeros_like(second)], axis=0)
-    return lax.dynamic_update_slice(both, second, (first.shape[0] + zero, 0, 0))
-
-
-def gather_blocks(block, devices, zero):
-    held = block
-    for bit in reversed(range(2, bit_count(devices))):
-        held = jnp.concatenate([held, exchange(held, bit, devices)], axis=0)
-    held = join(held, exchange(held, 1, devices), zero)
-    return held, exchange(held, 0, devices)
+def join_body(*refs):
+    count = len(refs) // 3
+    for at in range(count):
+        first, second, target = refs[2 * at], refs[2 * at + 1], refs[2 * count + at]
+        for block in range(first.shape[0]):
+            target[block] = first[block]
+            target[first.shape[0] + block] = second[block]
+
+
+def join(name, pairs, after=(), through=()):
+    outs = [((2 * first.shape[0], *first.shape[1:]), first.dtype) for first, _ in pairs]
+    return call_near(join_body, name, outs, [one for pair in pairs for one in pair], 1, after, through)
+
+
+def join_split_body(first, second, upper, lower):
+    rows = upper.shape[1]
+    for block in range(2 * first.shape[0]):
+        source = first if block < first.shape[0] else second
+        upper[block] = source[block % first.shape[0], 0:rows, :]
+        lower[block] = source[block % first.shape[0], rows:, :]
+
+
+def gather_both(self_held, cross_held, prepared, devices):
+    for bit in (4, 3, 2):
+        come = exchange(self_held, bit, devices)
+        (self_held,), _ = join(f"join_self_{bit}", [(self_held, come)], prepared if bit == 2 else ())
+    come = exchange(self_held, 1, devices)
+    cross_come = exchange(cross_held, 4, devices)
+    (cross_held,), _ = join("join_cross", [(cross_held, cross_come)])
+    cross_come = exchange(cross_held, 3, devices)
+    blocks, rows, width = cross_held.shape
+    (upper, lower), _ = call_near(
+        join_split_body, "join_split", [((2 * blocks, rows // 2, width), BF16)] * 2, [cross_held, cross_come], 1
+    )
+    upper_come, lower_come = exchange(upper, 2, devices), exchange(lower, 1, devices)
+    (upper, lower), _ = join("join_halves", [(upper, upper_come), (lower, lower_come)])
+    self_pieces = [self_held, come, exchange(self_held, 0, devices), exchange(come, 0, devices)]
+    return self_pieces, (upper, lower, exchange(upper, 1, devices), exchange(lower, 2, devices))
 
 
 def gather_plain(block, per, blocks):
@@ -794,10 +868,10 @@
     every = every.reshape(every.shape[0], parts, per, every.shape[2]).transpose(1, 0, 2, 3)
     every = every.reshape(parts, blocks, -1, every.shape[3]).transpose(1, 0, 2, 3)
     every = every.reshape(blocks, -1, every.shape[3])
-    return every[: blocks // 2], every[blocks // 2 :]
-
-
-def fold(name, groups, after=()):
+    return [every[at : at + blocks // 4] for at in range(0, blocks, blocks // 4)]
+
+
+def fold(name, groups, after=(), through=(), far=False):
     ins, outs, shapes = [], [], []
     for terms, axis in groups:
         high = max(row + kept.shape[-2] for kept, _, row, _ in terms)
@@ -808,8 +882,15 @@
             ins += [kept, came]
         outs += [((*lead, high, wide), BF16)] * 2
         shapes.append(([(row, column) for _, _, row, column in terms], axis))
-    results = call_near(lambda *refs: fold_body(shapes, *refs), name, outs, ins, 2, after)
-    return [tuple(results[at : at + 2]) for at in range(0, len(results), 2)]
+    after = [pltpu.with_memory_space_constraint(one, pltpu.HBM) for one in after]
+    near = range(1 if far else 0, len(ins), 2 if far else 1)
+    stay = range(1 if far == "both" else 0, len(outs), 2 if far == "both" else 1)
+    results = call(
+        lambda *refs: fold_body(shapes, *refs), name, outs, ins, (), 2, after=after, through=through, near=near, stay=stay,
+        limit=16,
+    )
+    passed = results[len(outs) :]
+    return [tuple(results[at : at + 2]) for at in range(0, len(outs), 2)] + list(passed)
 
 
 def local(
@@ -835,11 +916,11 @@
         spots = jnp.zeros((3,), jnp.int32)
 
     square, tall = (rows, width), (width, rows)
-    self_kaug, self_qaug, cross_kaug, cross_qaug, windows, prep_zero = call(
+    self_kaug, self_qaug, cross_kaug, cross_qaug, windows = call(
         prep_body, "prep",
-        [((rows, TILE), BF16), ((MASK_ROWS, rows), BF16)] * 2 + [((4, rows // TILE), jnp.int32), ((1,), jnp.int32)],
-        [tgt_lengths[0], tgt_pad, src_segments[0].reshape(-1, TILE), src_segments[0].reshape(-1, 1)],
-        (0, 1), 2, out_smem=(4, 5),
+        [((rows, TILE), BF16), ((MASK_ROWS, rows), BF16)] * 2 + [((4, rows // TILE), jnp.int32)],
+        [tgt_lengths[0], tgt_pad, src_segments[0].reshape(-1, TILE)],
+        (0, 1), 2, out_smem=(4,),
     )
     if direct:
         self_block, cross_block, ffn_block = call(
@@ -847,69 +928,69 @@
             [((1, 3 * BLOCK, width), BF16), ((1, 6 * BLOCK, width), BF16), ((parts * BLOCK + each, width), BF16)],
             [self_qkv, self_out, cross_qkv, cross_out, ffn_in, ffn_out, ln_gain, ln_bias], (), 1,
         )
-        self_low, self_high = gather_blocks(self_block, devices, prep_zero[0])
-        cross_held = cross_block
-        for bit in reversed(range(2, bit_count(devices))):
-            cross_held = jnp.concatenate([cross_held, exchange(cross_held, bit, devices)], axis=0)
-        cross_came = exchange(cross_held, 1, devices)
+        self_pieces, (upper, lower, upper_came, lower_came) = gather_both(self_block, cross_block, (self_kaug,), devices)
         ffn_all = lax.all_gather(ffn_block, AXES, axis=0, tiled=False)
     else:
         inner_rows = jnp.concatenate([ffn_in[:, at * width : (at + 1) * width] for at in range(parts)], axis=0)
         cross_block = jnp.concatenate([cross_qkv.reshape(-1, width), cross_out, self_out], axis=0)
-        self_low, self_high = gather_plain(self_qkv.reshape(-1, width), own, blocks)
-        cross_low, cross_high = gather_plain(cross_block, own, blocks)
+        self_pieces = gather_plain(self_qkv.reshape(-1, width), own, blocks)
+        cross_pieces = gather_plain(cross_block, own, blocks)
         scale_all = lax.all_gather(jnp.concatenate([ln_gain, ln_bias], axis=0), AXES, axis=1, tiled=True)
         scale_all = scale_all.reshape(-1, blocks, BLOCK).transpose(1, 0, 2)
         scale_all = jnp.pad(scale_all, ((0, 0), (0, BLOCK - scale_all.shape[1]), (0, width - BLOCK)))
-        cross_low = jnp.concatenate([cross_low, scale_all[: blocks // 2]], axis=1)
-        cross_high = jnp.concatenate([cross_high, scale_all[blocks // 2 :]], axis=1)
+        lower_pieces = [
+            jnp.concatenate([piece[:, 3 * BLOCK :], scale_all[at * blocks // 4 : (at + 1) * blocks // 4]], axis=1)
+            for at, piece in enumerate(cross_pieces)
+        ]
+        cross_pieces = [piece[:, : 3 * BLOCK] for piece in cross_pieces] + lower_pieces
         inner_all = jnp.concatenate(gather_plain(inner_rows, own, blocks), axis=0)
         outer_all = jnp.concatenate(gather_plain(ffn_out, ffn_out.shape[0], blocks), axis=0)
         ffn_all = jnp.concatenate([inner_all, outer_all], axis=1)
 
     halves, halves_t, masses = (2, rows, width // 2), (2, width // 2, rows), (2, 8, rows)
+    cross_ready = (upper, lower) if direct else ()
     saved = [(halves, BF16), (halves_t, BF16), (halves, BF16), (halves_t, BF16), (halves, BF16), (halves_t, BF16), (masses, F32)]
     pipeline = [(halves_t, BF16), ((2, rows, 2 * TILE), F32), ((2, rows, 2 * TILE), BF16)]
-    queries, queries_t, keys, keys_t, values, mixed_t, log_mass, weights, zero = call(
-        self_forward_body, "self_forward", saved + [((3, width, width), BF16), ((1,), jnp.int32)],
-        [self_low, self_high, token_rows, self_kaug, self_qaug, spots, windows],
-        (5, 6), 15, pipeline, out_smem=(8,), near=(0, 1), limit=44,
+    queries, queries_t, keys, keys_t, values, mixed_t, log_mass, weights = call(
+        self_forward_body, "self_forward", saved + [((3, width, width), BF16)],
+        [*self_pieces, token_rows, self_kaug, self_qaug, spots, windows],
+        (7, 8), 15, pipeline, after=cross_ready, limit=30,
     )
     if direct:
-        cross_low = join(cross_held, cross_came, zero[0])
-        cross_high = exchange(cross_low, 0, devices)
+        _, (upper_came, lower_came) = call_near(
+            lambda: None, "gate", [], [], 1, (mixed_t,), (upper_came, lower_came)
+        )
+        cross_pieces = [
+            upper, upper_came, exchange(upper, 0, devices), exchange(upper_came, 0, devices),
+            lower, lower_came, exchange(lower, 0, devices), exchange(lower_came, 0, devices),
+        ]
     (
         hidden_one, hidden_two, first_low, cross_queries, cross_queries_t, cross_keys, cross_keys_t, cross_values,
         cross_mixed_t, cross_mass, cross_weights, scales,
     ) = call(
         cross_forward_body, "cross_forward",
         [(square, F32)] * 2 + [(square, BF16)] + saved + [((5, width, width), BF16), ((BLOCK, width), F32)],
-        [cross_low, cross_high, token_rows, mixed_t, encoder_rows, cross_kaug, cross_qaug, spots, windows],
-        (7, 8), 18, pipeline + [(square, F32)], near=(0, 1), limit=50,
+        [*cross_pieces, token_rows, mixed_t, encoder_rows, cross_kaug, cross_qaug, spots, windows],
+        (13, 14), 18, pipeline + [(square, F32)], near=(3, 7) if direct else (), limit=40,
     )
     inside = parts * BLOCK + BLOCK
-    most = inside + each
-    result, grad_two, scale_grads, ffn_grads = call(
+    result, grad_two, scale_grads, inner_grads, outer_keep, outer_send = call(
         feed_forward_body, "feed_forward",
-        [(square, BF16), (square, F32), ((8, width), F32), ((blocks, most, width), BF16)],
+        [(square, BF16), (square, F32), ((8, width), F32), ((blocks, inside, width), BF16)]
+        + [((blocks // 2, each, width), BF16)] * 2,
         [ffn_all, hidden_two, out_grad[0], scales, cross_mixed_t, spots],
         (5,), 30,
         [
             ((width, wide), BF16), ((wide, width), BF16), ((wide, width), BF16), ((width, wide), BF16),
             (square, BF16), ((rows, wide), BF16), ((256, wide), F32), (square, BF16), ((rows, wide), BF16), (square, BF16),
-            ((8, 8, width), F32), ((blocks, most, width), BF16),
+            ((8, 8, width), F32), ((blocks, inside, width), BF16), ((blocks, each, width), BF16),
         ],
-        by_part=(3,),
+        by_part=(3, 4), stay=(5,),
     )
     if direct:
+        outer_came = exchange(outer_send, 0, devices)
         near_groups = [[8 * at + other for other in range(8)] for at in range(4)]
-        far_groups = [[at + 8 * other for other in range(4)] for at in range(8)]
-        ffn_sum = lax.psum_scatter(ffn_grads, AXES, scatter_dimension=0, axis_index_groups=near_groups, tiled=True)
-        ffn_sum = lax.psum_scatter(ffn_sum, AXES, scatter_dimension=0, axis_index_groups=far_groups, tiled=True)
-        ffn_sum = ffn_sum[0].astype(F32)
-        ffn_in_grad = jnp.concatenate([ffn_sum[at * BLOCK : (at + 1) * BLOCK] for at in range(parts)], axis=1)
-        cross_out_grad = ffn_sum[parts * BLOCK : inside]
-        ffn_out_grad = ffn_sum[inside:]
+        inner_sum = lax.psum_scatter(inner_grads, AXES, scatter_dimension=0, axis_index_groups=near_groups, tiled=True)
     work = [(halves, BF16), (halves_t, BF16), (masses, F32), (halves_t, F32), (halves, F32), (halves, F32)]
     grad_one, self_branch, cross_key_low, cross_value_low, cross_keep, cross_send = call(
         cross_backward_body, "cross_backward",
@@ -921,12 +1002,22 @@
         ],
         (18, 19), 25,
         [(square, BF16), (halves, BF16)] + work + [((2, 8, width), F32), ((blocks, 5 * BLOCK, width), BF16)],
-        by_part=(4, 5),
+        by_part=(4,), stay=(5,),
     )
 
     grid = (2, 2, 2, 2)
+    after = ()
     if direct:
+
+        def cube(value):
+            return value.reshape(grid + value.shape[1:])
+
+        (outer_keep, outer_send), cross_send = fold(
+            "fold_outer", [([(cube(outer_keep), cube(outer_came), 0, 0)], 0)], (self_branch,), (cross_send,), "both"
+        )
         cross_came = exchange(cross_send, 0, devices)
+        outer_came = exchange(outer_send, 1, devices)
+        after = (outer_send,)
     query_low, key_low, value_low, self_keep, self_send = call(
         self_backward_body, "self_backward",
         [(halves, BF16)] * 3 + [((blocks // 2, 3 * BLOCK, width), BF16)] * 2,
@@ -934,48 +1025,70 @@
             self_branch, (cross_weights, 4), mixed_t, queries_t, keys, self_kaug, self_qaug, values, log_mass, queries, keys_t,
             token_rows, windows, spots,
         ],
-        (12, 13), 25, work + [((blocks, 3 * BLOCK, width), BF16)], by_part=(3, 4),
+        (12, 13), 25, work + [((blocks, 3 * BLOCK, width), BF16)], after=after, by_part=(3,), stay=(4,), limit=36,
     )
     after = ()
     if direct:
-
-        def cube(value):
-            return value.reshape(grid + value.shape[1:])
-
+        (outer_keep, outer_send), (cross_keep, cross_send), self_send, inner_sum = fold(
+            "fold_first",
+            [([(outer_keep, outer_came, 0, 0)], 0), ([(cube(cross_keep), cube(cross_came), 0, 0)], 0)], (query_low,),
+            (self_send, pltpu.with_memory_space_constraint(inner_sum, pltpu.HBM)), "in",
+        )
         self_came = exchange(self_send, 0, devices)
-        ((cross_keep, cross_send),) = fold(
-            "fold_cross", [([(cube(cross_keep), cube(cross_came), 0, 0)], 0)], (query_low,)
+        inner_keep, inner_send = call(
+            order_body, "inner_order", [((2, inside, width), BF16)] * 2, [inner_sum, spots], (1,), 1, stay=(0, 1), limit=16,
         )
+        inner_came = exchange(inner_send, 3, devices)
+        outer_came = exchange(outer_send, 2, devices)
         cross_came = exchange(cross_send, 1, devices)
-        ((self_keep, self_send),) = fold("fold_self", [([(cube(self_keep), cube(self_came), 0, 0)], 1)], (cross_send,))
+        ((self_keep, self_send),) = fold(
+            "fold_self", [([(cube(self_keep), cube(self_came), 0, 0)], 1)], far="in"
+        )
         self_came = exchange(self_send, 2, devices)
         after = (cross_send, self_send)
     (encoder_grad,) = call(
         encoder_grad_body, "encoder_grad", [(square, BF16)],
-        [cross_key_low, cross_value_low, (cross_weights, slice(1, 3))], (), 4, after=after, limit=32,
+        [cross_key_low, cross_value_low, (cross_weights, slice(1, 3))], (), 4, after=after, limit=16,
     )
     if direct:
-        (cross_keep, cross_send), (self_keep, self_send) = fold(
-            "fold_second", [([(cross_keep, cross_came, 0, 0)], 0), ([(self_keep, self_came, 0, 0)], 0)], (encoder_grad,)
+        (inner_keep, inner_send), (cross_keep, cross_send), (self_keep, self_send) = fold(
+            "fold_second",
+            [
+                ([(inner_keep, inner_came, 0, 0)], 0), ([(cross_keep, cross_came, 0, 0)], 0),
+                ([(self_keep, self_came, 0, 0)], 0),
+            ],
+            (encoder_grad,),
         )
+        inner_came = exchange(inner_send, 4, devices)
         cross_came = exchange(cross_send, 2, devices)
         self_came = exchange(self_send, 1, devices)
         after = (cross_send, self_send)
     (tokens_grad,) = call(
         tokens_grad_body, "tokens_grad", [(square, BF16)], [grad_one, weights, query_low, key_low, value_low], (), 5,
-        after=after, limit=32,
+        after=after, limit=20,
     )
     if direct:
+        (ffn_in_grad, cross_out_grad), _ = call_near(
+            inner_total_body, "inner_total", [((own, wide), F32), ((own, width), F32)], [inner_keep, inner_came], 1,
+            stay=False,
+        )
         ((rest_keep, rest_send),) = fold(
-            "fold_third", [([(cross_keep, cross_came, 0, 0), (self_keep, self_came, 5 * BLOCK, 0)], 0)], (tokens_grad,)
+            "fold_third",
+            [
+                ([(cross_keep, cross_came, 0, 0), (self_keep, self_came, 5 * BLOCK, 0), (outer_keep, outer_came, 8 * BLOCK, 0)], 0),
+            ],
+            (tokens_grad, ffn_in_grad),
         )
         rest_came = exchange(rest_send, 3, devices)
         ((rest_keep, rest_send),) = fold("fold_fourth", [([(rest_keep, rest_came, 0, 0)], 0)])
         rest_came = exchange(rest_send, 4, devices)
-        cross_qkv_grad, self_out_grad, gain_grad, offset_grad, self_qkv_grad = call_near(
+        (cross_qkv_grad, self_out_grad, gain_grad, offset_grad, self_qkv_grad, ffn_out_grad), _ = call_near(
             total_body, "total",
-            [((3, own, width), F32), ((own, width), F32), ((3, own), F32), ((3, own), F32), ((3, own, width), F32)],
-            [rest_keep, rest_came], 1,
+            [
+                ((3, own, width), F32), ((own, width), F32), ((3, own), F32), ((3, own), F32), ((3, own, width), F32),
+                ((each, width), F32),
+            ],
+            [rest_keep, rest_came], 1, stay=False,
         )
     else:
 
@@ -986,10 +1099,10 @@
 
         cross_grads = jnp.concatenate([cross_keep, cross_send], axis=0)
         self_grads = jnp.concatenate([self_keep, self_send], axis=0)
-        inner_sum = add_up(ffn_grads, 0, parts * BLOCK, BLOCK)
+        inner_sum = add_up(inner_grads, 0, parts * BLOCK, BLOCK)
         ffn_in_grad = inner_sum.transpose(1, 0, 2).reshape(own, wide)
-        ffn_out_grad = add_up(ffn_grads, inside, most, each)[0]
-        cross_out_grad = add_up(ffn_grads, parts * BLOCK, inside, BLOCK)[0]
+        ffn_out_grad = add_up(jnp.concatenate([outer_keep, outer_send], axis=0), 0, each, each)[0]
+        cross_out_grad = add_up(inner_grads, parts * BLOCK, inside, BLOCK)[0]
         cross_qkv_grad = add_up(cross_grads, 0, 3 * BLOCK, BLOCK)
         self_out_grad = add_up(cross_grads, 3 * BLOCK, 4 * BLOCK, BLOCK)[0]
         scale_parts = cross_grads[:, 4 * BLOCK : 4 * BLOCK + 6, :BLOCK].astype(F32)

time: 249 us -> 232 us (0.932)
  local copies, waits for them, and re-layouts: 27.2 us -> 1.59 us
  starting transfers between devices: 23.1 us -> 37.3 us
  Pallas kernels: 122 us -> 132 us
  waiting for transfers between devices: 52.4 us -> 42.6 us
    unnamed x82 -> x26, local copies, waits for them, and re-layouts: 23.8 us -> 1.59 us
    ppermute x18 -> x29, starting transfers between devices: 23 us -> 37.3 us  [exchange_bit(): lax.ppermute(value, AXES, [(at, at ^ 1 << bit) for at in range(devices)])]
    ppermute x18 -> x29, waiting for transfers between devices: 52.3 us -> 42.5 us  [exchange_bit(): lax.ppermute(value, AXES, [(at, at ^ 1 << bit) for at in range(devices)])]
    pallas_call x9 -> x16, Pallas kernels: 121 us -> 130 us  [call(): pl.pallas_call(ordered, name=name, out_shape=[jax.ShapeDtypeStruct(shape,...]
  transfers between devices with their start and end apart: 21 -> 31, of which waited for: 11 -> 12; matrix products, arithmetic and copies ran while one was open for 1% -> 0% of each run, Pallas kernels for 38% -> 44%
where the time goes in v1:
time: 232 us; the launch traced here: 229 us
  Pallas kernels  132 us (57%)
  waiting for transfers between devices  42.6 us (18%)
  starting transfers between devices  37.3 us (16%)
  between operations  15.3 us (7%)
    pallas_call x16, Pallas kernels, call(): pl.pallas_call(ordered, name=name, out_shape=[jax.ShapeDtypeStruct(shape,...  130 us
    ppermute x29, waiting for transfers between devices, exchange_bit(): lax.ppermute(value, AXES, [(at, at ^ 1 << bit) for at in range(devices)])  42.5 us
    ppermute x29, starting transfers between devices, exchange_bit(): lax.ppermute(value, AXES, [(at, at ^ 1 << bit) for at in range(devices)])  37.3 us
  transfers between devices with their start and end apart: 31, of which 12 were waited for; matrix products, arithmetic and copies ran while one was open for 0% of the time, Pallas kernels for 44%

profile of v1, /device:TPU:0, one launch (start us, length us, event | category | flops | bytes accessed | tf_op | source)
XLA Modules:
  0.0 228.6 jit_solution(12740776084415767700)
XLA Ops:
  7.2 0.0 all-gather.3.cloned.1.call-start
  7.2 1.8 pack.1
  9.0 0.0 reduce-scatter.2.cloned.1.call-start
  9.1 4.1 %collective-permute-start.4 = (bf16[1,48,512]{2,1,0:T(8,128)(2,1)}, bf16[1,48,512]{2,1,0:T(8,128)(2,1)S(1)}, u32[]{:S(2)}, u32[]{:S(2)}) collective-permute-start(bf16[1,48,512]{2,1,0:T(8,128)(2,1)} %get-tuple-element.98.refs_0_), channel_id=1, source_target_pairs={{0,16},{1,17},{2,18},{3,19},{4,20},{5,21},{6,22},{7,23},{8,24},{9,... | collective-permute-start | bytes 147464 | tf_op jit(solution)/shard_map/across_zz/ppermute | solution.py:818
  13.2 2.8 %collective-permute-done.4.refs_1_ = bf16[1,48,512]{2,1,0:T(8,128)(2,1)S(1)} collective-permute-done((bf16[1,48,512]{2,1,0:T(8,128)(2,1)}, bf16[1,48,512]{2,1,0:T(8,128)(2,1)S(1)}, u32[]{:S(2)}, u32[]{:S(2)}) %collective-permute-start.4) | collective-permute-done | bytes 49184 | tf_op jit(solution)/shard_map/across_zz/ppermute | solution.py:818
  16.0 0.8 copy-done.6
  16.8 1.4 collective-permute-start.5
  18.3 3.2 %collective-permute-done.5.refs_1_ = bf16[2,48,512]{2,1,0:T(8,128)(2,1)S(1)} collective-permute-done((bf16[2,48,512]{2,1,0:T(8,128)(2,1)S(1)}, bf16[2,48,512]{2,1,0:T(8,128)(2,1)S(1)}, u32[]{:S(2)}, u32[]{:S(2)}) %collective-permute-start.5) | collective-permute-done | bytes 98336 | tf_op jit(solution)/shard_map/across_z/ppermute | solution.py:818
  21.5 1.8 collective-permute-start.6
  24.0 4.4 %prep.1 = (bf16[1024,128]{1,0:T(8,128)(2,1)}, bf16[32,1024]{1,0:T(8,128)(2,1)}, bf16[1024,128]{1,0:T(8,128)(2,1)}, bf16[32,1024]{1,0:T(8,128)(2,1)}, s32[4,8]{1,0:T(4,128)S(1)}) custom-call(s32[16]{0:T(128)S(1)} %bitcast.20, s32[1]{0:T(128)S(6)} %copy.35.refs_1_, s32[8,128]{1,0:T(8,128)} %bitcast.28), custom_call_target="tpu_custom_call" | custom-call | flops 2000000000 | tf_op jit(solution)/shard_map/prep/pallas_call | solution.py:112
  28.4 1.6 collective-permute-start.7
  30.0 2.2 collective-permute-start
  32.2 4.7 %collective-permute-done.refs_1_ = bf16[1,96,512]{2,1,0:T(8,128)(2,1)S(1)} collective-permute-done((bf16[1,96,512]{2,1,0:T(8,128)(2,1)S(1)}, bf16[1,96,512]{2,1,0:T(8,128)(2,1)S(1)}, u32[]{:S(2)}, u32[]{:S(2)}) %collective-permute-start) | collective-permute-done | bytes 98336 | tf_op jit(solution)/shard_map/across_zz/ppermute | solution.py:818
  37.0 0.1 collective-permute-start.1
  37.0 0.1 collective-permute-start.8
  37.1 0.5 collective-permute-start.9
  37.6 5.1 %collective-permute-done.1.refs_1_ = bf16[2,96,512]{2,1,0:T(8,128)(2,1)S(1)} collective-permute-done((bf16[2,96,512]{2,1,0:T(8,128)(2,1)S(1)}, bf16[2,96,512]{2,1,0:T(8,128)(2,1)S(1)}, u32[]{:S(2)}, u32[]{:S(2)}) %collective-permute-start.1) | collective-permute-done | bytes 196640 | tf_op jit(solution)/shard_map/across_z/ppermute | solution.py:818
  42.8 0.8 collective-permute-start.2
  43.6 0.5 collective-permute-start.3
  44.1 0.1 pad_add_fusion.refs_7_.refs_13_.refs_5_.refs_19_.refs_1_
  44.2 4.3 %collective-permute-done.2.refs_1_ = bf16[4,48,512]{2,1,0:T(8,128)(2,1)S(1)} collective-permute-done((bf16[4,48,512]{2,1,0:T(8,128)(2,1)S(1)}, bf16[4,48,512]{2,1,0:T(8,128)(2,1)S(1)}, u32[]{:S(2)}, u32[]{:S(2)}) %collective-permute-start.2) | collective-permute-done | bytes 196640 | tf_op jit(solution)/shard_map/across_y/ppermute | solution.py:818
  48.5 0.8 collective-permute-done.3.refs_3_
  49.3 0.1 join_halves.1
  49.4 0.1 collective-permute-start.12
  49.5 1.2 collective-permute-start.10
  50.7 0.2 collective-permute-start.14
  50.8 1.0 collective-permute-start.11
  51.9 0.7 copy-done.10
  52.6 16.1 %self_forward.1 = (bf16[2,1024,256]{2,1,0:T(8,128)(2,1)}, bf16[2,256,1024]{2,1,0:T(8,128)(2,1)}, bf16[2,1024,256]{2,1,0:T(8,128)(2,1)}, bf16[2,256,1024]{2,1,0:T...) custom-call(bf16[8,48,512]{2,1,0:T(8,128)(2,1)} %copy-done, ...), custom_call_target="tpu_custom_call" | custom-call | flops 15000000512 | tf_op jit(solution)/shard_map/self_forward/pallas_call | solution.py:112
  68.7 0.1 collective-permute-start.13
  68.9 0.4 collective-permute-start.15
  69.3 1.2 collective-permute-done.13.refs_3_
  70.5 0.6 collective-permute-done.15.refs_7_
  71.1 17.7 %cross_forward.1 = (f32[1024,512]{1,0:T(8,128)}, f32[1024,512]{1,0:T(8,128)}, bf16[1024,512]{1,0:T(8,128)(2,1)}, bf16[2,1024,256]{2,1,0:T(8,128)(2,1)}, bf16[2,2...) custom-call(bf16[8,48,512]{2,1,0:T(8,128)(2,1)} %copy-done.1, ...), custom_call_target="tpu_custom_call" | custom-call | flops 17999998976 | tf_op jit(solution)/shard_map/cross_forward/pallas_call | solution.py:112
  88.9 0.0 all-gather.3.cloned.1.call-done
  88.9 25.5 %feed_forward.1 = (bf16[1024,512]{1,0:T(8,128)(2,1)}, f32[1024,512]{1,0:T(8,128)}, f32[8,512]{1,0:T(8,128)}, bf16[32,80,512]{2,1,0:T(8,128)(2,1)}, bf16[16,64,51...) custom-call(bf16[32,128,512]{2,1,0:T(8,128)(2,1)} %bitcast.21, f32[1024,512]{1,0:T(8,128)} %get-tuple-element.108.refs_1_, ...), custom_call_target="tpu_custom_call" | custom-call | flops 30000001024 | tf_op jit(solution)/shard_map/feed_forward/pallas_call | solution.py:112
  114.4 0.1 collective-permute-start.16
  114.5 21.9 %cross_backward.1 = (f32[1024,512]{1,0:T(8,128)}, bf16[1024,512]{1,0:T(8,128)(2,1)}, bf16[2,1024,256]{2,1,0:T(8,128)(2,1)}, bf16[2,1024,256]{2,1,0:T(8,128)(2,1)...) custom-call(f32[1024,512]{1,0:T(8,128)} %get-tuple-element.112.refs_0_, ...), custom_call_target="tpu_custom_call" | custom-call | flops 24999999488 | tf_op jit(solution)/shard_map/cross_backward/pallas_call | solution.py:112
  136.4 2.4 %fold_outer.1 = (bf16[2,2,2,64,512]{4,3,2,1,0:T(8,128)(2,1)}, bf16[2,2,2,64,512]{4,3,2,1,0:T(8,128)(2,1)S(1)}, bf16[16,80,512]{2,1,0:T(8,128)(2,1)S(1)}) custom-call(bf16[2,2,2,2,64,512]{5,4,3,2,1,0:T(8,128)(2,1)} %bitcast.33, bf16[2,2,2,2,64,512]{5,4,3,2,1,0:T(8,128)(2,1)S(1)} %bitcast.18, ...), custom_call_target="tpu_custom_call", output_to_operand_aliasing={{2}: (3, {})} | custom-call | flops 2000000000 | tf_op jit(solution)/shard_map/fold_outer/pallas_call | solution.py:112
  138.8 1.9 collective-permute-start.17
  140.7 23.8 %self_backward.1 = (bf16[2,1024,256]{2,1,0:T(8,128)(2,1)}, bf16[2,1024,256]{2,1,0:T(8,128)(2,1)}, bf16[2,1024,256]{2,1,0:T(8,128)(2,1)}, bf16[16,48,512]{2,1,0:T(8,128)(2,1)}, bf16[16,48,512]{2,1,0:T(8,128)(2,1)S(1)}) custom-call(bf16[1024,512]{1,0:T(8,128)(2,1)} %get-tuple-element.125.refs_2_.refs_0_, ...), custom_call_target="tpu_custom_call" | custom-call | flops 24999999488 | tf_op jit(solution)/shard_map/self_backward/pallas_call | solution.py:112
  164.5 0.0 reduce-scatter.2.cloned.1.call-done.refs_6_
  164.5 1.9 fold_first.1
  166.4 0.6 collective-permute-start.21
  167.0 0.8 collective-permute-start.20
  167.7 1.2 collective-permute-done.21
  168.9 1.4 fold_self.1
  170.3 1.1 collective-permute-start.22
  171.4 1.6 inner_order.1
  173.0 7.4 %collective-permute-start.19 = (bf16[2,80,512]{2,1,0:T(8,128)(2,1)S(1)}, bf16[2,80,512]{2,1,0:T(8,128)(2,1)S(1)}, u32[]{:S(2)}, u32[]{:S(2)}) collective-permute-start(bf16[2,80,512]{2,1,0:T(8,128)(2,1)S(1)} %get-tuple-element.146), channel_id=1, source_target_pairs={{0,8},{1,9},{2,10},{3,11},{4,12},{5,13},{6,14},{7,15},{8,0},{9,1},... | collective-permute-start | bytes 491528 | tf_op jit(solution)/shard_map/across_z/ppermute | solution.py:818
  180.4 4.7 %encoder_grad.1.refs_6_ = bf16[1024,512]{1,0:T(8,128)(2,1)} custom-call(bf16[2,1024,256]{2,1,0:T(8,128)(2,1)} %get-tuple-element.153.refs_0_, bf16[2,1024,256]{2,1,0:T(8,128)(2,1)} %get-tuple-element.154.refs_1_, bf16[5,512,512]{2,1,0:T(8,128)(2,1)} %get-tuple-element.113.refs_1_.refs_11_.refs_2_, ...), custom_call_target="tpu_custom_call" | custom-call | flops 4000000000 | tf_op jit(solution)/shard_map/encoder_grad/pallas_call | solution.py:112
  185.1 0.3 fold_second.1
  185.5 6.8 %collective-permute-start.26 = (bf16[80,512]{1,0:T(8,128)(2,1)S(1)}, bf16[80,512]{1,0:T(8,128)(2,1)S(1)}, u32[]{:S(2)}, u32[]{:S(2)}) collective-permute-start(bf16[80,512]{1,0:T(8,128)(2,1)S(1)} %get-tuple-element.162), channel_id=1, source_target_pairs={{0,16},{1,17},{2,18},{3,19},{4,20},{5,21},{6,22},{7,23},{8,24},{9,... | collective-permute-start | bytes 245768 | tf_op jit(solution)/shard_map/across_zz/ppermute | solution.py:818
  192.3 1.7 collective-permute-start.24
  194.0 6.4 %tokens_grad.1.refs_6_ = bf16[1024,512]{1,0:T(8,128)(2,1)} custom-call(f32[1024,512]{1,0:T(8,128)} %get-tuple-element.123.refs_0_, bf16[3,512,512]{2,1,0:T(8,128)(2,1)} %get-tuple-element.124.refs_1_, bf16[2,1024,256]{2,1,0:T(8,128)(2,1)} %get-tuple-element.136.refs_4_.refs_2_, bf16[2,1024,256]{2,1,0:T(8,128)(2,1)} %get-tuple-element.137.refs_3_, ...), custom_call_target="tpu_custom_call" | custom-call | flops 5000000000 | tf_op jit(solution)/shard_map/tokens_grad/pallas_call | solution.py:112
  200.5 0.7 inner_total.1
  201.1 1.4 collective-permute-done.23.refs_1_
  202.5 0.2 fold_third.1
  202.7 0.1 collective-permute-start.27
  202.8 8.9 %collective-permute-done.27.refs_1_ = bf16[2,192,512]{2,1,0:T(8,128)(2,1)S(1)} collective-permute-done((bf16[2,192,512]{2,1,0:T(8,128)(2,1)S(1)}, bf16[2,192,512]{2,1,0:T(8,128)(2,1)S(1)}, u32[]{:S(2)}, u32[]{:S(2)}) %collective-permute-start.27) | collective-permute-done | bytes 393248 | tf_op jit(solution)/shard_map/across_z/ppermute | solution.py:818
  211.7 0.1 fold_fourth.1
  211.9 0.7 collective-permute-start.28
  212.6 8.3 %collective-permute-done.28.refs_1_ = bf16[192,512]{1,0:T(8,128)(2,1)S(1)} collective-permute-done((bf16[192,512]{1,0:T(8,128)(2,1)S(1)}, bf16[192,512]{1,0:T(8,128)(2,1)S(1)}, u32[]{:S(2)}, u32[]{:S(2)}) %collective-permute-start.28) | collective-permute-done | bytes 196640 | tf_op jit(solution)/shard_map/across_zz/ppermute | solution.py:818
  220.8 0.7 total.1
  (52 shorter events, 0.2 us)
Async XLA Ops:
  7.2 81.7 %all-gather.3.cloned.1.call-start = ((), (), s32[]{:S(2)}) async-start(), calls=%async_computation.2 | async-start | bytes 4325376 | tf_op jit(solution)/shard_map/all_gather | solution.py:932
  9.0 155.5 %reduce-scatter.2.cloned.1.call-start = ((), (), s32[]{:S(2)}) async-start(), calls=%async_computation.1 | async-start | bytes 2949120 | tf_op jit(solution)/shard_map/reduce_scatter | solution.py:993
  9.1 6.9 %collective-permute-start.4 = (bf16[1,48,512]{2,1,0:T(8,128)(2,1)}, bf16[1,48,512]{2,1,0:T(8,128)(2,1)S(1)}, u32[]{:S(2)}, u32[]{:S(2)}) collective-permute-start(bf16[1,48,512]{2,1,0:T(8,128)(2,1)} %get-tuple-element.98.refs_0_), channel_id=1, source_target_pairs={{0,16},{1,17},{2,18},{3,19},{4,20},{5,21},{6,22},{7,23},{8,24},{9,... | collective-permute-start | bytes 147464 | tf_op jit(solution)/shard_map/across_zz/ppermute | solution.py:818
  16.0 0.8 copy-start.6
  16.8 7.2 %copy-start.7 = (s32[1,16]{1,0:T(1,128)S(1)}, s32[1,16]{1,0:T(1,128)}, u32[]{:S(2)}) copy-start(s32[1,16]{1,0:T(1,128)} %param.25) | copy-start | bytes 196
  16.8 4.7 %collective-permute-start.5 = (bf16[2,48,512]{2,1,0:T(8,128)(2,1)S(1)}, bf16[2,48,512]{2,1,0:T(8,128)(2,1)S(1)}, u32[]{:S(2)}, u32[]{:S(2)}) collective-permute-start(bf16[2,48,512]{2,1,0:T(8,128)(2,1)S(1)} %join_self_4.1.refs_0_), channel_id=1, source_target_pairs={{0,8},{1,9},{2,10},{3,11},{4,12},{5,13},{6,14},{7,15},{8,0},{9,1},... | collective-permute-start | bytes 294920 | tf_op jit(solution)/shard_map/across_z/ppermute | solution.py:818
  21.5 6.8 %collective-permute-start.6 = (bf16[4,48,512]{2,1,0:T(8,128)(2,1)S(1)}, bf16[4,48,512]{2,1,0:T(8,128)(2,1)S(1)}, u32[]{:S(2)}, u32[]{:S(2)}) collective-permute-start(bf16[4,48,512]{2,1,0:T(8,128)(2,1)S(1)} %join_self_3.1.refs_0_), channel_id=1, source_target_pairs={{0,4},{1,5},{2,6},{3,7},{4,0},{5,1},{6,2},{7,3},{8,12},{9,13},{10,... | collective-permute-start | bytes 589832 | tf_op jit(solution)/shard_map/across_y/ppermute | solution.py:818
  28.3 1.7 copy-start.5
  28.4 14.4 %copy-start = (bf16[8,48,512]{2,1,0:T(8,128)(2,1)}, bf16[8,48,512]{2,1,0:T(8,128)(2,1)S(1)}, u32[]{:S(2)}) copy-start(bf16[8,48,512]{2,1,0:T(8,128)(2,1)S(1)} %join_self_2.1.refs_0_) | copy-start | bytes 1179652
  28.4 8.7 %collective-permute-start.7 = (bf16[8,48,512]{2,1,0:T(8,128)(2,1)S(1)}, bf16[8,48,512]{2,1,0:T(8,128)(2,1)S(1)}, u32[]{:S(2)}, u32[]{:S(2)}) collective-permute-start(bf16[8,48,512]{2,1,0:T(8,128)(2,1)S(1)} %join_self_2.1.refs_0_), channel_id=1, source_target_pairs={{0,2},{1,3},{2,0},{3,1},{4,6},{5,7},{6,4},{7,5},{8,10},{9,11},{10,... | collective-permute-start | bytes 1179656 | tf_op jit(solution)/shard_map/across_x/ppermute | solution.py:818
  30.0 7.0 %collective-permute-start = (bf16[1,96,512]{2,1,0:T(8,128)(2,1)S(1)}, bf16[1,96,512]{2,1,0:T(8,128)(2,1)S(1)}, u32[]{:S(2)}, u32[]{:S(2)}) collective-permute-start(bf16[1,96,512]{2,1,0:T(8,128)(2,1)S(1)} %copy-done.5), channel_id=1, source_target_pairs={{0,16},{1,17},{2,18},{3,19},{4,20},{5,21},{6,22},{7,23},{8,24},{9,... | collective-permute-start | bytes 294920 | tf_op jit(solution)/shard_map/across_zz/ppermute | solution.py:818
  37.0 5.8 %collective-permute-start.1 = (bf16[2,96,512]{2,1,0:T(8,128)(2,1)S(1)}, bf16[2,96,512]{2,1,0:T(8,128)(2,1)S(1)}, u32[]{:S(2)}, u32[]{:S(2)}) collective-permute-start(bf16[2,96,512]{2,1,0:T(8,128)(2,1)S(1)} %join_cross.1.refs_0_), channel_id=1, source_target_pairs={{0,8},{1,9},{2,10},{3,11},{4,12},{5,13},{6,14},{7,15},{8,0},{9,1},... | collective-permute-start | bytes 589832 | tf_op jit(solution)/shard_map/across_z/ppermute | solution.py:818
  37.0 13.8 %collective-permute-start.8 = (bf16[8,48,512]{2,1,0:T(8,128)(2,1)S(1)}, bf16[8,48,512]{2,1,0:T(8,128)(2,1)S(1)}, u32[]{:S(2)}, u32[]{:S(2)}) collective-permute-start(bf16[8,48,512]{2,1,0:T(8,128)(2,1)S(1)} %join_self_2.1.refs_0_), channel_id=1, source_target_pairs={{0,1},{1,0},{2,3},{3,2},{4,5},{5,4},{6,7},{7,6},{8,9},{9,8},{10,11... | collective-permute-start | bytes 1179656 | tf_op jit(solution)/shard_map/across_core/ppermute | solution.py:818
  37.1 12.2 %copy-start.8 = (bf16[8,48,512]{2,1,0:T(8,128)(2,1)}, bf16[8,48,512]{2,1,0:T(8,128)(2,1)S(1)}, u32[]{:S(2)}) copy-start(bf16[8,48,512]{2,1,0:T(8,128)(2,1)S(1)} %collective-permute-done.7.refs_1_) | copy-start | bytes 1179652
  37.1 14.7 %collective-permute-start.9 = (bf16[8,48,512]{2,1,0:T(8,128)(2,1)S(1)}, bf16[8,48,512]{2,1,0:T(8,128)(2,1)S(1)}, u32[]{:S(2)}, u32[]{:S(2)}) collective-permute-start(bf16[8,48,512]{2,1,0:T(8,128)(2,1)S(1)} %collective-permute-done.7.refs_1_), channel_id=1, source_target_pairs={{0,1},{1,0},{2,3},{3,2},{4,5},{5,4},{6,7},{7,6},{8,9},{9,8},{10,11... | collective-permute-start | bytes 1179656 | tf_op jit(solution)/shard_map/across_core/ppermute | solution.py:818
  42.8 5.7 %collective-permute-start.2 = (bf16[4,48,512]{2,1,0:T(8,128)(2,1)S(1)}, bf16[4,48,512]{2,1,0:T(8,128)(2,1)S(1)}, u32[]{:S(2)}, u32[]{:S(2)}) collective-permute-start(bf16[4,48,512]{2,1,0:T(8,128)(2,1)S(1)} %get-tuple-element.95.refs_0_), channel_id=1, source_target_pairs={{0,4},{1,5},{2,6},{3,7},{4,0},{5,1},{6,2},{7,3},{8,12},{9,13},{10,... | collective-permute-start | bytes 589832 | tf_op jit(solution)/shard_map/across_y/ppermute | solution.py:818
  43.6 5.7 %collective-permute-start.3 = (bf16[4,48,512]{2,1,0:T(8,128)(2,1)S(1)}, bf16[4,48,512]{2,1,0:T(8,128)(2,1)S(1)}, u32[]{:S(2)}, u32[]{:S(2)}) collective-permute-start(bf16[4,48,512]{2,1,0:T(8,128)(2,1)S(1)} %get-tuple-element.96.refs_2_), channel_id=1, source_target_pairs={{0,2},{1,3},{2,0},{3,1},{4,6},{5,7},{6,4},{7,5},{8,10},{9,11},{10,... | collective-permute-start | bytes 589832 | tf_op jit(solution)/shard_map/across_x/ppermute | solution.py:818
  49.3 19.3 %copy-start.1 = (bf16[8,48,512]{2,1,0:T(8,128)(2,1)}, bf16[8,48,512]{2,1,0:T(8,128)(2,1)S(1)}, u32[]{:S(2)}) copy-start(bf16[8,48,512]{2,1,0:T(8,128)(2,1)S(1)} %get-tuple-element.97.refs_9_.refs_0_) | copy-start | bytes 1179652
  49.4 19.3 %copy-start.2 = (bf16[8,48,512]{2,1,0:T(8,128)(2,1)}, bf16[8,48,512]{2,1,0:T(8,128)(2,1)S(1)}, u32[]{:S(2)}) copy-start(bf16[8,48,512]{2,1,0:T(8,128)(2,1)S(1)} %get-tuple-element.102.refs_10_.refs_4_) | copy-start | bytes 1179652
  49.4 19.9 %collective-permute-start.12 = (bf16[8,48,512]{2,1,0:T(8,128)(2,1)S(1)}, bf16[8,48,512]{2,1,0:T(8,128)(2,1)S(1)}, u32[]{:S(2)}, u32[]{:S(2)}) collective-permute-start(bf16[8,48,512]{2,1,0:T(8,128)(2,1)S(1)} %get-tuple-element.97.refs_9_.refs_0_), channel_id=1, source_target_pairs={{0,1},{1,0},{2,3},{3,2},{4,5},{5,4},{6,7},{7,6},{8,9},{9,8},{10,11... | collective-permute-start | bytes 1179656 | tf_op jit(solution)/shard_map/across_core/ppermute | solution.py:818
  49.5 19.2 %collective-permute-start.10 = (bf16[8,48,512]{2,1,0:T(8,128)(2,1)S(1)}, bf16[8,48,512]{2,1,0:T(8,128)(2,1)S(1)}, u32[]{:S(2)}, u32[]{:S(2)}) collective-permute-start(bf16[8,48,512]{2,1,0:T(8,128)(2,1)S(1)} %get-tuple-element.97.refs_9_.refs_0_), channel_id=1, source_target_pairs={{0,2},{1,3},{2,0},{3,1},{4,6},{5,7},{6,4},{7,5},{8,10},{9,11},{10,... | collective-permute-start | bytes 1179656 | tf_op jit(solution)/shard_map/across_x/ppermute | solution.py:818
  50.7 18.6 %collective-permute-start.14 = (bf16[8,48,512]{2,1,0:T(8,128)(2,1)S(1)}, bf16[8,48,512]{2,1,0:T(8,128)(2,1)S(1)}, u32[]{:S(2)}, u32[]{:S(2)}) collective-permute-start(bf16[8,48,512]{2,1,0:T(8,128)(2,1)S(1)} %get-tuple-element.102.refs_10_.refs_4_), channel_id=1, source_target_pairs={{0,1},{1,0},{2,3},{3,2},{4,5},{5,4},{6,7},{7,6},{8,9},{9,8},{10,11... | collective-permute-start | bytes 1179656 | tf_op jit(solution)/shard_map/across_core/ppermute | solution.py:818
  50.8 1.0 copy-start.9
  50.8 17.9 %collective-permute-start.11 = (bf16[8,48,512]{2,1,0:T(8,128)(2,1)S(1)}, bf16[8,48,512]{2,1,0:T(8,128)(2,1)S(1)}, u32[]{:S(2)}, u32[]{:S(2)}) collective-permute-start(bf16[8,48,512]{2,1,0:T(8,128)(2,1)S(1)} %get-tuple-element.102.refs_10_.refs_4_), channel_id=1, source_target_pairs={{0,4},{1,5},{2,6},{3,7},{4,0},{5,1},{6,2},{7,3},{8,12},{9,13},{10,... | collective-permute-start | bytes 1179656 | tf_op jit(solution)/shard_map/across_y/ppermute | solution.py:818
  51.9 0.7 copy-start.10
  68.7 2.4 %copy-start.3 = (bf16[8,48,512]{2,1,0:T(8,128)(2,1)}, bf16[8,48,512]{2,1,0:T(8,128)(2,1)S(1)}, u32[]{:S(2)}) copy-start(bf16[8,48,512]{2,1,0:T(8,128)(2,1)S(1)} %get-tuple-element.104.refs_1_) | copy-start | bytes 1179652
  68.7 2.4 %copy-start.4 = (bf16[8,48,512]{2,1,0:T(8,128)(2,1)}, bf16[8,48,512]{2,1,0:T(8,128)(2,1)S(1)}, u32[]{:S(2)}) copy-start(bf16[8,48,512]{2,1,0:T(8,128)(2,1)S(1)} %get-tuple-element.105.refs_5_) | copy-start | bytes 1179652
  68.7 1.8 collective-permute-start.13
  68.9 2.2 collective-permute-start.15
  69.3 1.8 copy-start.11
  69.3 1.8 copy-start.12
  114.4 22.0 %collective-permute-start.16 = (bf16[16,64,512]{2,1,0:T(8,128)(2,1)S(1)}, bf16[16,64,512]{2,1,0:T(8,128)(2,1)S(1)}, u32[]{:S(2)}, u32[]{:S(2)}) collective-permute-start(bf16[16,64,512]{2,1,0:T(8,128)(2,1)S(1)} %get-tuple-element.133), channel_id=1, source_target_pairs={{0,1},{1,0},{2,3},{3,2},{4,5},{5,4},{6,7},{7,6},{8,9},{9,8},{10,11... | collective-permute-start | bytes 3145736 | tf_op jit(solution)/shard_map/across_core/ppermute | solution.py:818
  138.8 25.7 %collective-permute-start.17 = (bf16[2,2,2,64,512]{4,3,2,1,0:T(8,128)(2,1)S(1)}, bf16[2,2,2,64,512]{4,3,2,1,0:T(8,128)(2,1)S(1)}, u32[]{:S(2)}, u32[]{:S(2)}) collective-permute-start(bf16[2,2,2,64,512]{4,3,2,1,0:T(8,128)(2,1)S(1)} %get-tuple-element.135.refs_14_), channel_id=1, source_target_pairs={{0,2},{1,3},{2,0},{3,1},{4,6},{5,7},{6,4},{7,5},{8,10},{9,11},{10,... | collective-permute-start | bytes 1572872 | tf_op jit(solution)/shard_map/across_x/ppermute | solution.py:818
  140.7 23.8 %collective-permute-start.18 = (bf16[16,80,512]{2,1,0:T(8,128)(2,1)S(1)}, bf16[16,80,512]{2,1,0:T(8,128)(2,1)S(1)}, u32[]{:S(2)}, u32[]{:S(2)}) collective-permute-start(bf16[16,80,512]{2,1,0:T(8,128)(2,1)S(1)} %get-tuple-element.141), channel_id=1, source_target_pairs={{0,1},{1,0},{2,3},{3,2},{4,5},{5,4},{6,7},{7,6},{8,9},{9,8},{10,11... | collective-permute-start | bytes 3932168 | tf_op jit(solution)/shard_map/across_core/ppermute | solution.py:818
  166.4 2.5 %collective-permute-start.21 = (bf16[16,48,512]{2,1,0:T(8,128)(2,1)S(1)}, bf16[16,48,512]{2,1,0:T(8,128)(2,1)S(1)}, u32[]{:S(2)}, u32[]{:S(2)}) collective-permute-start(bf16[16,48,512]{2,1,0:T(8,128)(2,1)S(1)} %get-tuple-element.150), channel_id=1, source_target_pairs={{0,1},{1,0},{2,3},{3,2},{4,5},{5,4},{6,7},{7,6},{8,9},{9,8},{10,11... | collective-permute-start | bytes 2359304 | tf_op jit(solution)/shard_map/across_core/ppermute | solution.py:818
  167.0 18.2 %collective-permute-start.20 = (bf16[2,2,2,80,512]{4,3,2,1,0:T(8,128)(2,1)S(1)}, bf16[2,2,2,80,512]{4,3,2,1,0:T(8,128)(2,1)S(1)}, u32[]{:S(2)}, u32[]{:S(2)}) collective-permute-start(bf16[2,2,2,80,512]{4,3,2,1,0:T(8,128)(2,1)S(1)} %get-tuple-element.148.refs_3_), channel_id=1, source_target_pairs={{0,2},{1,3},{2,0},{3,1},{4,6},{5,7},{6,4},{7,5},{8,10},{9,11},{10,... | collective-permute-start | bytes 1966088 | tf_op jit(solution)/shard_map/across_x/ppermute | solution.py:818
  170.3 14.9 %collective-permute-start.22 = (bf16[2,2,2,48,512]{4,3,2,1,0:T(8,128)(2,1)S(1)}, bf16[2,2,2,48,512]{4,3,2,1,0:T(8,128)(2,1)S(1)}, u32[]{:S(2)}, u32[]{:S(2)}) collective-permute-start(bf16[2,2,2,48,512]{4,3,2,1,0:T(8,128)(2,1)S(1)} %get-tuple-element.152.refs_4_), channel_id=1, source_target_pairs={{0,4},{1,5},{2,6},{3,7},{4,0},{5,1},{6,2},{7,3},{8,12},{9,13},{10,... | collective-permute-start | bytes 1179656 | tf_op jit(solution)/shard_map/across_y/ppermute | solution.py:818
  173.0 12.1 %collective-permute-start.19 = (bf16[2,80,512]{2,1,0:T(8,128)(2,1)S(1)}, bf16[2,80,512]{2,1,0:T(8,128)(2,1)S(1)}, u32[]{:S(2)}, u32[]{:S(2)}) collective-permute-start(bf16[2,80,512]{2,1,0:T(8,128)(2,1)S(1)} %get-tuple-element.146), channel_id=1, source_target_pairs={{0,8},{1,9},{2,10},{3,11},{4,12},{5,13},{6,14},{7,15},{8,0},{9,1},... | collective-permute-start | bytes 491528 | tf_op jit(solution)/shard_map/across_z/ppermute | solution.py:818
  180.3 20.8 %collective-permute-start.25 = (bf16[2,2,64,512]{3,2,1,0:T(8,128)(2,1)S(1)}, bf16[2,2,64,512]{3,2,1,0:T(8,128)(2,1)S(1)}, u32[]{:S(2)}, u32[]{:S(2)}) collective-permute-start(bf16[2,2,64,512]{3,2,1,0:T(8,128)(2,1)S(1)} %get-tuple-element.160), channel_id=1, source_target_pairs={{0,4},{1,5},{2,6},{3,7},{4,0},{5,1},{6,2},{7,3},{8,12},{9,13},{10,... | collective-permute-start | bytes 786440 | tf_op jit(solution)/shard_map/across_y/ppermute | solution.py:818
  185.5 15.0 %collective-permute-start.26 = (bf16[80,512]{1,0:T(8,128)(2,1)S(1)}, bf16[80,512]{1,0:T(8,128)(2,1)S(1)}, u32[]{:S(2)}, u32[]{:S(2)}) collective-permute-start(bf16[80,512]{1,0:T(8,128)(2,1)S(1)} %get-tuple-element.162), channel_id=1, source_target_pairs={{0,16},{1,17},{2,18},{3,19},{4,20},{5,21},{6,22},{7,23},{8,24},{9,... | collective-permute-start | bytes 245768 | tf_op jit(solution)/shard_map/across_zz/ppermute | solution.py:818
  192.3 8.8 %collective-permute-start.24 = (bf16[2,2,48,512]{3,2,1,0:T(8,128)(2,1)S(1)}, bf16[2,2,48,512]{3,2,1,0:T(8,128)(2,1)S(1)}, u32[]{:S(2)}, u32[]{:S(2)}) collective-permute-start(bf16[2,2,48,512]{3,2,1,0:T(8,128)(2,1)S(1)} %get-tuple-element.156.refs_6_), channel_id=1, source_target_pairs={{0,2},{1,3},{2,0},{3,1},{4,6},{5,7},{6,4},{7,5},{8,10},{9,11},{10,... | collective-permute-start | bytes 589832 | tf_op jit(solution)/shard_map/across_x/ppermute | solution.py:818
  194.0 8.5 %collective-permute-start.23 = (bf16[2,2,80,512]{3,2,1,0:T(8,128)(2,1)S(1)}, bf16[2,2,80,512]{3,2,1,0:T(8,128)(2,1)S(1)}, u32[]{:S(2)}, u32[]{:S(2)}) collective-permute-start(bf16[2,2,80,512]{3,2,1,0:T(8,128)(2,1)S(1)} %get-tuple-element.155.refs_5_), channel_id=1, source_target_pairs={{0,4},{1,5},{2,6},{3,7},{4,0},{5,1},{6,2},{7,3},{8,12},{9,13},{10,... | collective-permute-start | bytes 983048 | tf_op jit(solution)/shard_map/across_y/ppermute | solution.py:818
  202.7 9.0 %collective-permute-start.27 = (bf16[2,192,512]{2,1,0:T(8,128)(2,1)S(1)}, bf16[2,192,512]{2,1,0:T(8,128)(2,1)S(1)}, u32[]{:S(2)}, u32[]{:S(2)}) collective-permute-start(bf16[2,192,512]{2,1,0:T(8,128)(2,1)S(1)} %get-tuple-element.165), channel_id=1, source_target_pairs={{0,8},{1,9},{2,10},{3,11},{4,12},{5,13},{6,14},{7,15},{8,0},{9,1},... | collective-permute-start | bytes 1179656 | tf_op jit(solution)/shard_map/across_z/ppermute | solution.py:818
  211.9 9.0 %collective-permute-start.28 = (bf16[192,512]{1,0:T(8,128)(2,1)S(1)}, bf16[192,512]{1,0:T(8,128)(2,1)S(1)}, u32[]{:S(2)}, u32[]{:S(2)}) collective-permute-start(bf16[192,512]{1,0:T(8,128)(2,1)S(1)} %get-tuple-element.167), channel_id=1, source_target_pairs={{0,16},{1,17},{2,18},{3,19},{4,20},{5,21},{6,22},{7,23},{8,24},{9,... | collective-permute-start | bytes 589832 | tf_op jit(solution)/shard_map/across_zz/ppermute | solution.py:818
Sparse Core Ops, SparseCore 0:
  11.4 67.2 all-gather.2
  114.5 49.6 reduce-scatter.1
